TPU v7x, 256 devices: a whole 4x4x8 slice. The times are simulated.
256 devices in a mesh: energy: 64 (over z, y_lo, x), mom: 4 (over y_hi, core).
Axes of the slice: x: 4, y: 4 (y_hi: 2, y_lo: 2; y = y_hi * 2 + y_lo), z: 8, core: 2. Of those that a mesh axis runs over, the one named last changes fastest.
Arguments:
- green_lesser: bfloat16 [64, 4, 2, 512, 512], P('energy', 'mom'), may hold values from -6 to 6
- coupling: bfloat16 [4, 512, 512], replicated, may hold values from -0.25 to 0.25
- offsets: int32 [4], replicated, may hold values from 1 to 4, as said below
- occupation: float32 [4], replicated, may hold values from 0.05 to 2
- transfer_weight: float32 [4, 4], replicated, may hold values from 0.2 to 1
- transfer_table: int32 [4, 4], replicated, may hold values from 0 to 3, as said below
Outputs:
- sigma_lesser: bfloat16 [64, 4, 2, 512, 512], P('energy', 'mom')
Inputs may be any that keep to these rules, and one draw needn't show every extreme that they name: The 4 offsets are distinct. `transfer_table`: each row names every momentum once.
All inputs are finite; a program needn't handle non-finite values.
Results may differ from a plain program's by a relative error of at most 0.0058.
Values may be sent and summed in bfloat16 or wider, within the bound.
No kernel may reach another device: no remote copies, remote signals or barrier semaphores. Data moves between devices by JAX's collectives and lax.ppermute only.
A program may use at most 64 MiB of HBM per device.

v0:
```python
import jax
import jax.numpy as jnp
from jax import lax
from jax.sharding import PartitionSpec as P

MAXOFF = 4


def passed_along(value, axis, steps):
    count = lax.axis_size(axis)
    leading, last = (max(0, -steps), min(count, count - steps))
    return lax.ppermute(value, axis, [(source, source + steps) for source in range(leading, last)])


def shards(green_lesser, coupling, offsets, occupation, transfer_weight, transfer_table):
    local_count = green_lesser.shape[1]
    lower = []
    upper = []
    for dist in range(1, MAXOFF + 1):
        lower.append(passed_along(green_lesser, "energy", dist))
        upper.append(passed_along(green_lesser, "energy", -dist))
    low_stack = jnp.concatenate(lower, axis=0)
    high_stack = jnp.concatenate(upper, axis=0)
    picks = offsets - 1
    low_pick = jnp.take(low_stack, picks, axis=0)
    high_pick = jnp.take(high_stack, picks, axis=0)
    weight_low = occupation[:, None, None, None, None]
    weight_high = weight_low + 1.0
    shifted = (
        weight_low * low_pick.astype(jnp.float32) + weight_high * high_pick.astype(jnp.float32)
    ).astype(jnp.bfloat16)
    left = jnp.einsum(
        "vij,vkpjl->vkpil", coupling, shifted, preferred_element_type=jnp.float32
    ).astype(jnp.bfloat16)
    term = jnp.einsum("vkpil,vml->vkpim", left, coupling, preferred_element_type=jnp.float32)
    own_index = lax.axis_index("mom") * local_count + jnp.arange(local_count, dtype=jnp.int32)
    onehot = (transfer_table[:, :, None] == own_index[None, None, :]).astype(jnp.float32)
    mixing = jnp.einsum("qv,kqj->vkj", transfer_weight, onehot, precision=lax.Precision.HIGHEST)
    summed = lax.psum_scatter(
        jnp.einsum("vkj,vjpim->kpim", mixing, term, precision=lax.Precision.HIGHEST),
        "mom",
        scatter_dimension=0,
        tiled=True,
    )
    return summed[None].astype(jnp.bfloat16)


def solution(mesh):
    return jax.shard_map(
        shards,
        mesh=mesh,
        in_specs=(P("energy", "mom", None, None, None), P(), P(), P(), P(), P()),
        out_specs=P("energy", "mom", None, None, None),
        check_vma=False,
    )
```

profile of v0, /device:TPU:129, one launch (start us, length us, event | category | flops | bytes accessed | tf_op | source)
XLA Modules:
  0.0 358.3 jit_solution(18404351863687229035)
XLA Ops:
  6.5 3.2 collective-permute-start
  9.8 4.4 %collective-permute-start.1 = (bf16[1,1,2,512,512]{4,3,2,1,0:T(8,128)(2,1)}, bf16[1,1,2,512,512]{4,3,2,1,0:T(8,128)(2,1)}, u32[]{:S(2)}, u32[]{:S(2)}) collective-permute-start(bf16[1,1,2,512,512]{4,3,2,1,0:T(8,128)(2,1)} %param.8), channel_id=1, source_target_pairs={{0,8},{4,12},{8,16},{12,20},{16,24},{20,28},{24,32},{28,36},{32,40... | collective-permute-start | bytes 3145736 | tf_op jit(solution)/shard_map/ppermute | solution.py:12
  14.2 4.1 %collective-permute-start.2 = (bf16[1,1,2,512,512]{4,3,2,1,0:T(8,128)(2,1)}, bf16[1,1,2,512,512]{4,3,2,1,0:T(8,128)(2,1)}, u32[]{:S(2)}, u32[]{:S(2)}) collective-permute-start(bf16[1,1,2,512,512]{4,3,2,1,0:T(8,128)(2,1)} %param.8), channel_id=1, source_target_pairs={{0,12},{4,16},{8,20},{12,24},{16,28},{20,32},{24,36},{28,40},{32,4... | collective-permute-start | bytes 3145736 | tf_op jit(solution)/shard_map/ppermute | solution.py:12
  18.2 2.5 collective-permute-start.3
  20.8 4.6 %collective-permute-start.4 = (bf16[1,1,2,512,512]{4,3,2,1,0:T(8,128)(2,1)}, bf16[1,1,2,512,512]{4,3,2,1,0:T(8,128)(2,1)S(1)}, u32[]{:S(2)}, u32[]{:S(2)}) collective-permute-start(bf16[1,1,2,512,512]{4,3,2,1,0:T(8,128)(2,1)} %param.8), channel_id=1, source_target_pairs={{4,0},{8,4},{12,8},{16,12},{20,16},{24,20},{28,24},{32,28},{36,32}... | collective-permute-start | bytes 3145736 | tf_op jit(solution)/shard_map/ppermute | solution.py:12
  25.4 62.1 %collective-permute-done = bf16[1,1,2,512,512]{4,3,2,1,0:T(8,128)(2,1)} collective-permute-done((bf16[1,1,2,512,512]{4,3,2,1,0:T(8,128)(2,1)}, bf16[1,1,2,512,512]{4,3,2,1,0:T(8,128)(2,1)}, u32[]{:S(2)}, u32[]{:S(2)}) %collective-permute-start) | collective-permute-done | bytes 1048608 | tf_op jit(solution)/shard_map/ppermute | solution.py:12
  87.5 1.9 collective-permute-start.5
  89.4 10.3 %collective-permute-done.1 = bf16[1,1,2,512,512]{4,3,2,1,0:T(8,128)(2,1)} collective-permute-done((bf16[1,1,2,512,512]{4,3,2,1,0:T(8,128)(2,1)}, bf16[1,1,2,512,512]{4,3,2,1,0:T(8,128)(2,1)}, u32[]{:S(2)}, u32[]{:S(2)}) %collective-permute-start.1) | collective-permute-done | bytes 1048608 | tf_op jit(solution)/shard_map/ppermute | solution.py:12
  99.7 1.9 collective-permute-start.6
  101.7 45.4 %collective-permute-start.7 = (bf16[1,1,2,512,512]{4,3,2,1,0:T(8,128)(2,1)}, bf16[1,1,2,512,512]{4,3,2,1,0:T(8,128)(2,1)}, u32[]{:S(2)}, u32[]{:S(2)}) collective-permute-start(bf16[1,1,2,512,512]{4,3,2,1,0:T(8,128)(2,1)} %param.8), channel_id=1, source_target_pairs={{16,0},{20,4},{24,8},{28,12},{32,16},{36,20},{40,24},{44,28},{48,3... | collective-permute-start | bytes 3145736 | tf_op jit(solution)/shard_map/ppermute | solution.py:12
  147.1 0.7 compare_and_fusion
  147.7 0.8 convolution_bitcast_fusion
  148.6 0.7 broadcast_add_fusion
  149.2 3.7 %maximum_bitcast_fusion = bf16[4,2,512,512]{3,2,1,0:T(8,128)(2,1)} fusion(bf16[1,1,2,512,512]{4,3,2,1,0:T(8,128)(2,1)} %collective-permute-done.3, bf16[1,1,2,512,512]{4,3,2,1,0:T(8,128)(2,1)} %collective-permute-done.2, bf16[1,1,2,512,512]{4,3,2,1,0:T(8,128)(2,1)} %collective-permute-done.1, bf16[1,1,2,512,512]{4,3,2,1,0:T(8,128)(2,1)} %collective-permute-done), kind=kLoop, calls=%fused_computation.7 | loop fusion | flops 6291456 | bytes 8388608 | tf_op jit(solution)/shard_map/jit(_take)/Arg_0.3 | solution.py:25
  152.9 5.0 %gather_fusion = bf16[4,2,512,512]{3,2,1,0:T(8,128)(2,1)} fusion(bf16[4,2,512,512]{3,2,1,0:T(8,128)(2,1)} %maximum_bitcast_fusion, s32[1024]{0:T(1024)S(1)} %pad_clamp_fusion), kind=kCustom, calls=%fused_computation.clone | custom fusion | bytes 8388624 | tf_op jit(solution)/shard_map/jit(_take)/gather | solution.py:25
  157.9 8.9 %collective-permute-done.7 = bf16[1,1,2,512,512]{4,3,2,1,0:T(8,128)(2,1)} collective-permute-done((bf16[1,1,2,512,512]{4,3,2,1,0:T(8,128)(2,1)}, bf16[1,1,2,512,512]{4,3,2,1,0:T(8,128)(2,1)}, u32[]{:S(2)}, u32[]{:S(2)}) %collective-permute-start.7) | collective-permute-done | bytes 1048608 | tf_op jit(solution)/shard_map/ppermute | solution.py:12
  166.9 3.5 maximum_bitcast_fusion.1
  170.4 4.9 %gather_fusion.1 = bf16[4,2,512,512]{3,2,1,0:T(8,128)(2,1)} fusion(bf16[4,2,512,512]{3,2,1,0:T(8,128)(2,1)} %maximum_bitcast_fusion.1, s32[1024]{0:T(1024)S(1)} %pad_clamp_fusion), kind=kCustom, calls=%fused_computation.1.clone | custom fusion | bytes 8388624 | tf_op jit(solution)/shard_map/jit(_take)/gather | solution.py:26
  175.3 10.8 %fusion.5 = f32[4,2,512,512]{3,2,1,0:T(8,128)} fusion(bf16[4,512,512]{2,1,0:T(8,128)(2,1)S(1)} %copy-done, bf16[4,2,512,512]{3,2,1,0:T(8,128)(2,1)} %gather_fusion.1, bf16[4,2,512,512]{3,2,1,0:T(8,128)(2,1)} %gather_fusion, f32[4]{0:T(128)S(1)} %broadcast_add_fusion, f32[4]{0:T(128)S(1)} %copy-done.1, pred[4]{0:T(512)(128)(4,1)S(1)} %get-tuple-element.6), kind=kOutput, calls=%fused_computation.9 | convolution fusion | flops 4313841664 | bytes 18874404 | tf_op jit(solution)/shard_map/vkpil,vml->vkpim/dot_general | solution.py:35
  186.1 25.7 %fusion = f32[4,2,512,512]{3,0,2,1:T(4,128)S(1)} fusion(f32[4,4,1,1]{1,0,3,2:T(4,128)S(1)} %convolution_bitcast_fusion, f32[4,2,512,512]{3,2,1,0:T(8,128)} %fusion.5), kind=kOutput, calls=%fused_computation.2 | convolution fusion | flops 100663296 | bytes 16777280 | tf_op jit(solution)/shard_map/vkj,vjpim->kpim/dot_general | solution.py:40
  211.9 5.8 %copy.12 = f32[4,2,512,512]{3,2,1,0:T(8,128)} copy(f32[4,2,512,512]{3,0,2,1:T(4,128)S(1)} %fusion) | data formatting | bytes 16777216 | tf_op jit(solution)/shard_map/vkj,vjpim->kpim/dot_general | solution.py:40
  217.6 0.0 reduce-scatter.2.cloned.1.call-update
  217.7 131.1 %reduce-scatter.2.cloned.1.call-done = f32[1,2,512,512]{3,2,1,0:T(8,128)} async-done(((f32[4,2,512,512]{3,2,1,0:T(8,128)}), f32[1,2,512,512]{3,2,1,0:T(8,128)}) %reduce-scatter.2.cloned.1.call-update) | async-done | bytes 2097168 | tf_op jit(solution)/shard_map/reduce_scatter | solution.py:39
  348.8 2.7 convert_bitcast_fusion
  (11 shorter events, 0.0 us)
Async XLA Ops:
  6.5 168.8 %copy-start = (bf16[4,512,512]{2,1,0:T(8,128)(2,1)S(1)}, bf16[4,512,512]{2,1,0:T(8,128)(2,1)}, u32[]{:S(2)}) copy-start(bf16[4,512,512]{2,1,0:T(8,128)(2,1)} %param.9) | copy-start | bytes 6291460
  6.5 342.3 %reduce-scatter.2.cloned.1.call-start = ((), (), s32[]{:S(2)}) async-start(), calls=%async_computation.1 | async-start | bytes 10485760 | tf_op jit(solution)/shard_map/reduce_scatter | solution.py:39
  6.5 81.0 %collective-permute-start = (bf16[1,1,2,512,512]{4,3,2,1,0:T(8,128)(2,1)}, bf16[1,1,2,512,512]{4,3,2,1,0:T(8,128)(2,1)}, u32[]{:S(2)}, u32[]{:S(2)}) collective-permute-start(bf16[1,1,2,512,512]{4,3,2,1,0:T(8,128)(2,1)} %param.8), channel_id=1, source_target_pairs={{0,4},{4,8},{8,12},{12,16},{16,20},{20,24},{24,28},{28,32},{32,36}... | collective-permute-start | bytes 3145736 | tf_op jit(solution)/shard_map/ppermute | solution.py:12
  9.8 90.0 %collective-permute-start.1 = (bf16[1,1,2,512,512]{4,3,2,1,0:T(8,128)(2,1)}, bf16[1,1,2,512,512]{4,3,2,1,0:T(8,128)(2,1)}, u32[]{:S(2)}, u32[]{:S(2)}) collective-permute-start(bf16[1,1,2,512,512]{4,3,2,1,0:T(8,128)(2,1)} %param.8), channel_id=1, source_target_pairs={{0,8},{4,12},{8,16},{12,20},{16,24},{20,28},{24,32},{28,36},{32,40... | collective-permute-start | bytes 3145736 | tf_op jit(solution)/shard_map/ppermute | solution.py:12
  14.2 87.5 %collective-permute-start.2 = (bf16[1,1,2,512,512]{4,3,2,1,0:T(8,128)(2,1)}, bf16[1,1,2,512,512]{4,3,2,1,0:T(8,128)(2,1)}, u32[]{:S(2)}, u32[]{:S(2)}) collective-permute-start(bf16[1,1,2,512,512]{4,3,2,1,0:T(8,128)(2,1)} %param.8), channel_id=1, source_target_pairs={{0,12},{4,16},{8,20},{12,24},{16,28},{20,32},{24,36},{28,40},{32,4... | collective-permute-start | bytes 3145736 | tf_op jit(solution)/shard_map/ppermute | solution.py:12
  18.2 131.0 %collective-permute-start.3 = (bf16[1,1,2,512,512]{4,3,2,1,0:T(8,128)(2,1)}, bf16[1,1,2,512,512]{4,3,2,1,0:T(8,128)(2,1)}, u32[]{:S(2)}, u32[]{:S(2)}) collective-permute-start(bf16[1,1,2,512,512]{4,3,2,1,0:T(8,128)(2,1)} %param.8), channel_id=1, source_target_pairs={{0,16},{4,20},{8,24},{12,28},{16,32},{20,36},{24,40},{28,44},{32,4... | collective-permute-start | bytes 3145736 | tf_op jit(solution)/shard_map/ppermute | solution.py:12
  20.8 137.1 %collective-permute-start.4 = (bf16[1,1,2,512,512]{4,3,2,1,0:T(8,128)(2,1)}, bf16[1,1,2,512,512]{4,3,2,1,0:T(8,128)(2,1)S(1)}, u32[]{:S(2)}, u32[]{:S(2)}) collective-permute-start(bf16[1,1,2,512,512]{4,3,2,1,0:T(8,128)(2,1)} %param.8), channel_id=1, source_target_pairs={{4,0},{8,4},{12,8},{16,12},{20,16},{24,20},{28,24},{32,28},{36,32}... | collective-permute-start | bytes 3145736 | tf_op jit(solution)/shard_map/ppermute | solution.py:12
  87.5 70.4 %collective-permute-start.5 = (bf16[1,1,2,512,512]{4,3,2,1,0:T(8,128)(2,1)}, bf16[1,1,2,512,512]{4,3,2,1,0:T(8,128)(2,1)}, u32[]{:S(2)}, u32[]{:S(2)}) collective-permute-start(bf16[1,1,2,512,512]{4,3,2,1,0:T(8,128)(2,1)} %param.8), channel_id=1, source_target_pairs={{8,0},{12,4},{16,8},{20,12},{24,16},{28,20},{32,24},{36,28},{40,32... | collective-permute-start | bytes 3145736 | tf_op jit(solution)/shard_map/ppermute | solution.py:12
  99.7 58.2 %collective-permute-start.6 = (bf16[1,1,2,512,512]{4,3,2,1,0:T(8,128)(2,1)}, bf16[1,1,2,512,512]{4,3,2,1,0:T(8,128)(2,1)}, u32[]{:S(2)}, u32[]{:S(2)}) collective-permute-start(bf16[1,1,2,512,512]{4,3,2,1,0:T(8,128)(2,1)} %param.8), channel_id=1, source_target_pairs={{12,0},{16,4},{20,8},{24,12},{28,16},{32,20},{36,24},{40,28},{44,3... | collective-permute-start | bytes 3145736 | tf_op jit(solution)/shard_map/ppermute | solution.py:12
  101.7 65.2 %collective-permute-start.7 = (bf16[1,1,2,512,512]{4,3,2,1,0:T(8,128)(2,1)}, bf16[1,1,2,512,512]{4,3,2,1,0:T(8,128)(2,1)}, u32[]{:S(2)}, u32[]{:S(2)}) collective-permute-start(bf16[1,1,2,512,512]{4,3,2,1,0:T(8,128)(2,1)} %param.8), channel_id=1, source_target_pairs={{16,0},{20,4},{24,8},{28,12},{32,16},{36,20},{40,24},{44,28},{48,3... | collective-permute-start | bytes 3145736 | tf_op jit(solution)/shard_map/ppermute | solution.py:12
  170.4 4.9 %copy-start.1 = (f32[4]{0:T(128)S(1)}, f32[4]{0:T(128)}, u32[]{:S(2)}) copy-start(f32[4]{0:T(128)} %param.11) | copy-start | bytes 52
Sparse Core Ops, SparseCore 0:
  217.8 130.9 reduce-scatter.1
where the time goes:
time: 361 us; the launch traced here: 358 us
  waiting for transfers between devices  213 us (59%)
  starting transfers between devices  68 us (19%)
  matrix products  37.3 us (10%)
  local copies, waits for them, and re-layouts  15.7 us (4%)
  between operations  13.5 us (4%)
  other arithmetic  11.3 us (3%)
    reduce_scatter x1, waiting for transfers between devices, shards(): lax.psum_scatter(jnp.einsum('vkj,vjpim->kpim', mixing, term, precision=la...  131 us
    ppermute x8, waiting for transfers between devices, passed_along(): lax.ppermute(value, axis, [(source, source + steps) for source in range(l...  81.4 us
    ppermute x8, starting transfers between devices, passed_along(): lax.ppermute(value, axis, [(source, source + steps) for source in range(l...  68 us
    dot_general x1, matrix products, shards(): jnp.einsum('vkj,vjpim->kpim', mixing, term, precision=lax.Precision.HIGHEST)  25.7 us
    dot_general x1, matrix products, shards(): jnp.einsum('vkpil,vml->vkpim', left, coupling, preferred_element_type=jnp...  10.8 us
  transfers between devices with their start and end apart: 9, of which 4 were waited for; matrix products, arithmetic and copies ran while one was open for 3% of the time, Pallas kernels for 0%

commit v1 on v0

v1 whole, which is shorter than its diff:
```python
import functools
import jax
import jax.numpy as jnp
from jax import lax
from jax.experimental import pallas as pl
from jax.experimental.pallas import tpu as pltpu
from jax.sharding import Mesh, PartitionSpec as P

PLANES, ROWS, XS, HALVES, CORES = 8, 2, 4, 2, 2
PLANE = ("lo", "x", "hi", "core")
NE = ROWS * XS
NK = HALVES * CORES
NV = 4
NO = 512
SLICES = NE * NK
DEPTH = 2 * NO // SLICES
HALO = 4


def mix_kernel(offsets, occupation, weight, table, below, own, above, out, raw, mixing):
    raw[0:HALO] = below[...].reshape(HALO, NK, DEPTH, NO).astype(jnp.float32)
    raw[HALO : HALO + NE] = own[...].reshape(NE, NK, DEPTH, NO).astype(jnp.float32)
    raw[HALO + NE :] = above[...].reshape(HALO, NK, DEPTH, NO).astype(jnp.float32)
    for k in range(NK):
        for q in range(NK):
            for v in range(NV):
                mixing[v, k, table[k, q]] = weight[q, v]

    def step(index, carry):
        v = index // NE
        e = index % NE
        off = offsets[v]
        low = occupation[v]
        high = low + 1.0
        for part in range(DEPTH // 16):
            rows = slice(part * 16, part * 16 + 16)
            shifted = [
                low * raw[e + HALO - off, j, rows, :] + high * raw[e + HALO + off, j, rows, :]
                for j in range(NK)
            ]
            for k in range(NK):
                total = mixing[v, k, 0] * shifted[0]
                for j in range(1, NK):
                    total = total + mixing[v, k, j] * shifted[j]
                out[e * NK + k, v, rows, :] = total.astype(jnp.bfloat16)
        return carry

    lax.fori_loop(0, NV * NE, step, 0)


def mixed(offsets, occupation, weight, table, below, own, above):
    smem = pl.BlockSpec(memory_space=pltpu.SMEM)
    vmem = pl.BlockSpec(memory_space=pltpu.VMEM)
    return pl.pallas_call(
        mix_kernel,
        out_shape=jax.ShapeDtypeStruct((SLICES, NV, DEPTH, NO), jnp.bfloat16),
        in_specs=[smem] * 4 + [vmem] * 3,
        out_specs=vmem,
        scratch_shapes=[
            pltpu.VMEM((NE + 2 * HALO, NK, DEPTH, NO), jnp.float32),
            pltpu.SMEM((NV, NK, NK), jnp.float32),
        ],
        compiler_params=pltpu.CompilerParams(vmem_limit_bytes=24 << 20),
    )(offsets, occupation, weight, table, below, own, above)


def product_kernel(coupling, shifted, out):
    for part in range(2):
        total = None
        for v in range(NV):
            block = shifted[part * 16 : part * 16 + 16, v].reshape(NO, NO)
            left = jnp.dot(coupling[v], block, preferred_element_type=jnp.float32)
            term = lax.dot_general(
                left.astype(jnp.bfloat16),
                coupling[v],
                (((1,), (1,)), ((), ())),
                preferred_element_type=jnp.float32,
            )
            total = term if total is None else total + term
        out[part] = total.astype(jnp.bfloat16)


def products(coupling, shifted):
    vmem = pl.BlockSpec(memory_space=pltpu.VMEM)
    return pl.pallas_call(
        product_kernel,
        out_shape=jax.ShapeDtypeStruct((2, NO, NO), jnp.bfloat16),
        in_specs=[vmem] * 2,
        out_specs=vmem,
        compiler_params=pltpu.CompilerParams(vmem_limit_bytes=32 << 20),
    )(coupling, shifted)


def shards(green_lesser, coupling, offsets, occupation, transfer_weight, transfer_table):
    slices = green_lesser.reshape(SLICES, DEPTH, NO)
    own = lax.all_to_all(slices, PLANE, 0, 0, tiled=True)
    half = SLICES // 2
    below = lax.ppermute(own[half:], "z", [(z, z + 1) for z in range(PLANES - 1)])
    above = lax.ppermute(own[:half], "z", [(z + 1, z) for z in range(PLANES - 1)])
    out = mixed(offsets, occupation, transfer_weight, transfer_table, below, own, above)
    shifted = lax.all_to_all(out.reshape(SLICES, NV * DEPTH, NO), PLANE, 0, 0, tiled=True)
    sigma = products(coupling, shifted.reshape(SLICES, NV, DEPTH, NO))
    return sigma[None, None]


def solution(mesh):
    fine = Mesh(
        mesh.devices.reshape(PLANES, ROWS, XS, HALVES, CORES),
        ("z", "lo", "x", "hi", "core"),
    )
    split = P(("z", "lo", "x"), ("hi", "core"), None, None, None)
    return jax.shard_map(
        shards,
        mesh=fine,
        in_specs=(split, P(), P(), P(), P(), P()),
        out_specs=split,
        check_vma=False,
    )
```

time: 361 us -> 109 us (0.30)
  waiting for transfers between devices: 213 us -> 12.6 us
  blocking collectives: 0 us -> 80.4 us
  starting transfers between devices: 68 us -> 5.28 us
  matrix products: 37.3 us -> 0 us
  local copies, waits for them, and re-layouts: 15.7 us -> 0.09 us
  between operations: 13.5 us -> 0.06 us
  other arithmetic: 11.3 us -> 0 us
  Pallas kernels: 0 us -> 9.82 us
    reduce_scatter x1 -> x0, waiting for transfers between devices: 131 us -> none  [shards(): lax.psum_scatter(jnp.einsum('vkj,vjpim->kpim', mixing, term, precision=la...]
    all_to_all x0 -> x2, blocking collectives: none -> 80.4 us  [the longest x1 55.3 us: shards(): lax.all_to_all(out.reshape(SLICES, NV * DEPTH, NO), PLANE, 0, 0, tiled=True)]
    ppermute x8 -> x2, waiting for transfers between devices: 81.4 us -> 12.6 us  [the longest x1 9.62 us: shards(): lax.ppermute(own[:half], 'z', [(z + 1, z) for z in range(PLANES - 1)])]
    ppermute x8 -> x2, starting transfers between devices: 68 us -> 5.28 us  [the longest x1 3.36 us: shards(): lax.ppermute(own[half:], 'z', [(z, z + 1) for z in range(PLANES - 1)])]
    dot_general x3 -> x0, matrix products: 37.3 us -> none  [the longest x1 25.7 us: shards(): jnp.einsum('vkj,vjpim->kpim', mixing, term, precision=lax.Precision.HIGHEST)]
    gather x2 -> x0, local copies, waits for them, and re-layouts: 9.9 us -> none  [the longest x1 4.96 us: shards(): low_pick = jnp.take(low_stack, picks, axis=0)]
    pallas_call x0 -> x2, Pallas kernels: none -> 9.82 us  [the longest x1 5.48 us: products(): pl.pallas_call(product_kernel, out_shape=jax.ShapeDtypeStruct((2, NO, NO)...]
    another operation x2 -> x0, other arithmetic: 7.25 us -> none  [the longest x1 3.71 us: shards(): low_pick = jnp.take(low_stack, picks, axis=0)]
  transfers between devices with their start and end apart: 9 -> 2, of which waited for: 4 -> 2; matrix products, arithmetic and copies ran while one was open for 3% -> 0% of each run, Pallas kernels for 0% -> 0%
where the time goes in v1:
time: 109 us; the launch traced here: 108 us
  blocking collectives  80.4 us (74%)
  waiting for transfers between devices  12.6 us (12%)
  Pallas kernels  9.82 us (9%)
  starting transfers between devices  5.28 us (5%)
    all_to_all x1, blocking collectives, shards(): lax.all_to_all(out.reshape(SLICES, NV * DEPTH, NO), PLANE, 0, 0, tiled=True)  55.3 us
    all_to_all x1, blocking collectives, shards(): own = lax.all_to_all(slices, PLANE, 0, 0, tiled=True)  25.1 us
    ppermute x1, waiting for transfers between devices, shards(): lax.ppermute(own[:half], 'z', [(z + 1, z) for z in range(PLANES - 1)])  9.62 us
    pallas_call x1, Pallas kernels, products(): pl.pallas_call(product_kernel, out_shape=jax.ShapeDtypeStruct((2, NO, NO)...  5.48 us
    pallas_call x1, Pallas kernels, mixed(): pl.pallas_call(mix_kernel, out_shape=jax.ShapeDtypeStruct((SLICES, NV, DE...  4.34 us
    ppermute x1, starting transfers between devices, shards(): lax.ppermute(own[half:], 'z', [(z, z + 1) for z in range(PLANES - 1)])  3.36 us
    ppermute x1, waiting for transfers between devices, shards(): lax.ppermute(own[half:], 'z', [(z, z + 1) for z in range(PLANES - 1)])  3.03 us
  transfers between devices with their start and end apart: 2, of which 2 were waited for; matrix products, arithmetic and copies ran while one was open for 0% of the time, Pallas kernels for 0%

profile of v1, /device:TPU:129, one launch (start us, length us, event | category | flops | bytes accessed | tf_op | source)
XLA Modules:
  0.0 108.3 jit_solution(3076571506121304879)
XLA Ops:
  0.0 0.0 copy-start.2
  0.0 0.0 copy-start.1
  0.0 0.0 copy-start.4
  0.0 0.0 copy-start.3
  0.0 25.1 %all_to_all.10.own = bf16[32,32,512]{2,1,0:T(8,128)(2,1)S(1)} all-to-all(bf16[32,32,512]{2,1,0:T(8,128)(2,1)} %bitcast.6), channel_id=1, replica_groups=mesh['z'=8,'lo'=2,'x'=4,'hi'=2,'core'=2] {'lo','x','hi','core'}, dimensions={0} | all-to-all | bytes 2097152 | tf_op jit(solution)/shard_map/all_to_all | solution.py:96
  25.1 0.1 fusion
  25.1 1.9 %collective-permute-start.1 = (bf16[16,32,512]{2,1,0:T(8,128)(2,1)S(1)}, bf16[16,32,512]{2,1,0:T(8,128)(2,1)S(1)}, u32[]{:S(2)}, u32[]{:S(2)}) collective-permute-start(bf16[16,32,512]{2,1,0:T(8,128)(2,1)S(1)} %get-tuple-element.5), channel_id=1, source_target_pairs={{32,0},{64,32},{96,64},{128,96},{160,128},{192,160},{224,192},{33,... | collective-permute-start | bytes 1572872 | tf_op jit(solution)/shard_map/ppermute | solution.py:99
  27.1 3.4 %collective-permute-start = (bf16[16,32,512]{2,1,0:T(8,128)(2,1)S(1)}, bf16[16,32,512]{2,1,0:T(8,128)(2,1)S(1)}, u32[]{:S(2)}, u32[]{:S(2)}) collective-permute-start(bf16[16,32,512]{2,1,0:T(8,128)(2,1)S(1)} %get-tuple-element.6), channel_id=1, source_target_pairs={{0,32},{32,64},{64,96},{96,128},{128,160},{160,192},{192,224},{1,3... | collective-permute-start | bytes 1572872 | tf_op jit(solution)/shard_map/ppermute | solution.py:98
  30.4 9.6 %collective-permute-done.1.above = bf16[16,32,512]{2,1,0:T(8,128)(2,1)S(1)} collective-permute-done((bf16[16,32,512]{2,1,0:T(8,128)(2,1)S(1)}, bf16[16,32,512]{2,1,0:T(8,128)(2,1)S(1)}, u32[]{:S(2)}, u32[]{:S(2)}) %collective-permute-start.1) | collective-permute-done | bytes 524320 | tf_op jit(solution)/shard_map/ppermute | solution.py:99
  40.1 3.0 %collective-permute-done.below = bf16[16,32,512]{2,1,0:T(8,128)(2,1)S(1)} collective-permute-done((bf16[16,32,512]{2,1,0:T(8,128)(2,1)S(1)}, bf16[16,32,512]{2,1,0:T(8,128)(2,1)S(1)}, u32[]{:S(2)}, u32[]{:S(2)}) %collective-permute-start) | collective-permute-done | bytes 524320 | tf_op jit(solution)/shard_map/ppermute | solution.py:98
  43.1 0.0 copy-done.2
  43.1 0.0 copy-done.1
  43.1 0.0 copy-done.4
  43.1 0.0 copy-done.3
  43.1 4.3 %shard_map.64 = bf16[32,4,32,512]{3,2,1,0:T(8,128)(2,1)S(1)} custom-call(s32[4]{0:T(128)S(1)} %copy-done.3, f32[4]{0:T(128)S(1)} %copy-done.4, f32[4,4]{1,0:T(4,128)S(1)} %copy-done.1, s32[4,4]{1,0:T(4,128)S(1)} %copy-done.2, bf16[16,32,512]{2,1,0:T(8,128)(2,1)S(1)} %collective-permute-done.below, bf16[32,32,512]{2,1,0:T(8,128)(2,1)S(1)} %all_to_all.10.own, ...), custom_call_target="tpu_custom_call" | custom-call | tf_op jit(solution)/shard_map/pallas_call | solution.py:54
  47.5 0.0 copy-start
  47.5 55.3 %all_to_all.11 = bf16[32,128,512]{2,1,0:T(8,128)(2,1)S(1)} all-to-all(bf16[32,128,512]{2,1,0:T(8,128)(2,1)S(1)} %bitcast.5), channel_id=1, replica_groups=mesh['z'=8,'lo'=2,'x'=4,'hi'=2,'core'=2] {'lo','x','hi','core'}, dimensions={0} | all-to-all | bytes 8388608 | tf_op jit(solution)/shard_map/all_to_all | solution.py:101
  102.8 0.0 copy-done
  102.8 5.5 %shard_map.65 = bf16[2,512,512]{2,1,0:T(8,128)(2,1)} custom-call(bf16[4,512,512]{2,1,0:T(8,128)(2,1)S(1)} %copy-done, bf16[32,4,32,512]{3,2,1,0:T(8,128)(2,1)S(1)} %bitcast.4), custom_call_target="tpu_custom_call" | custom-call | tf_op jit(solution)/shard_map/pallas_call | solution.py:85
Async XLA Ops:
  0.0 43.1 %copy-start.2 = (s32[4,4]{1,0:T(4,128)S(1)}, s32[4,4]{1,0:T(4,128)}, u32[]{:S(2)}) copy-start(s32[4,4]{1,0:T(4,128)} %table.1) | copy-start | bytes 196
  0.0 43.1 %copy-start.1 = (f32[4,4]{1,0:T(4,128)S(1)}, f32[4,4]{1,0:T(4,128)}, u32[]{:S(2)}) copy-start(f32[4,4]{1,0:T(4,128)} %weight.1) | copy-start | bytes 196
  0.0 43.1 %copy-start.4 = (f32[4]{0:T(128)S(1)}, f32[4]{0:T(128)}, u32[]{:S(2)}) copy-start(f32[4]{0:T(128)} %occupation.1) | copy-start | bytes 52
  0.0 43.1 %copy-start.3 = (s32[4]{0:T(128)S(1)}, s32[4]{0:T(128)}, u32[]{:S(2)}) copy-start(s32[4]{0:T(128)} %offsets.1) | copy-start | bytes 52
  25.1 14.9 %collective-permute-start.1 = (bf16[16,32,512]{2,1,0:T(8,128)(2,1)S(1)}, bf16[16,32,512]{2,1,0:T(8,128)(2,1)S(1)}, u32[]{:S(2)}, u32[]{:S(2)}) collective-permute-start(bf16[16,32,512]{2,1,0:T(8,128)(2,1)S(1)} %get-tuple-element.5), channel_id=1, source_target_pairs={{32,0},{64,32},{96,64},{128,96},{160,128},{192,160},{224,192},{33,... | collective-permute-start | bytes 1572872 | tf_op jit(solution)/shard_map/ppermute | solution.py:99
  27.1 16.0 %collective-permute-start = (bf16[16,32,512]{2,1,0:T(8,128)(2,1)S(1)}, bf16[16,32,512]{2,1,0:T(8,128)(2,1)S(1)}, u32[]{:S(2)}, u32[]{:S(2)}) collective-permute-start(bf16[16,32,512]{2,1,0:T(8,128)(2,1)S(1)} %get-tuple-element.6), channel_id=1, source_target_pairs={{0,32},{32,64},{64,96},{96,128},{128,160},{160,192},{192,224},{1,3... | collective-permute-start | bytes 1572872 | tf_op jit(solution)/shard_map/ppermute | solution.py:98
  47.5 55.3 %copy-start = (bf16[4,512,512]{2,1,0:T(8,128)(2,1)S(1)}, bf16[4,512,512]{2,1,0:T(8,128)(2,1)}, u32[]{:S(2)}) copy-start(bf16[4,512,512]{2,1,0:T(8,128)(2,1)} %coupling.1) | copy-start | bytes 6291460

commit v2 on v1

v2 whole, which is shorter than its diff:
```python
import jax
import jax.numpy as jnp
from jax import lax
from jax.experimental import pallas as pl
from jax.experimental.pallas import tpu as pltpu
from jax.sharding import Mesh, PartitionSpec as P

PLANES, ROWS, XS, HALVES, CORES = 8, 2, 4, 2, 2
PLANE = ("lo", "x", "hi", "core")
NE = ROWS * XS
NK = HALVES * CORES
NV = 4
NO = 512
SLICES = NE * NK
DEPTH = 2 * NO // SLICES
HALO = 4
WIDE = NK * DEPTH


def weight_kernel(offsets, occupation, weight, table, out, mixing):
    for k in range(NK):
        for q in range(NK):
            for v in range(NV):
                mixing[v, k, table[k, q]] = weight[q, v]
    row = lax.broadcasted_iota(jnp.int32, (DEPTH, WIDE), 0)
    column = lax.broadcasted_iota(jnp.int32, (DEPTH, WIDE), 1)
    for v in range(NV):
        for k in range(NK):
            base = jnp.zeros((DEPTH, WIDE), jnp.float32)
            for j in range(NK):
                base = jnp.where(column == row + DEPTH * j, mixing[v, k, j], base)
            for side in range(2):
                scaled = base * (occupation[v] + float(side))
                high = scaled.astype(jnp.bfloat16)
                rest = (scaled - high.astype(jnp.float32)).astype(jnp.bfloat16)
                columns = slice(side * WIDE, (side + 1) * WIDE)
                out[v, k * DEPTH : (k + 1) * DEPTH, columns] = high
                out[v, WIDE + k * DEPTH : WIDE + (k + 1) * DEPTH, columns] = rest


def mix(offsets, scale, out, sources, energies):
    for dist in range(1, HALO + 1):
        mode = jnp.int32(0)
        for v in range(1, NV):
            mode = jnp.where(offsets[v] == dist, v, mode)
        for e in energies(dist):
            pair = jnp.concatenate([sources(e - dist), sources(e + dist)], axis=0)
            total = jnp.dot(scale[mode], pair, preferred_element_type=jnp.float32)
            total = (total[:WIDE] + total[WIDE:]).astype(jnp.bfloat16)
            for k in range(NK):
                out[e * NK + k, mode] = total[k * DEPTH : (k + 1) * DEPTH]


def inner(dist):
    return range(dist, NE - dist)


def outer(dist):
    return [e for e in range(NE) if e not in inner(dist)]


def inner_kernel(offsets, scale, own, out):
    mix(offsets, scale, out, lambda e: own[e * NK : (e + 1) * NK].reshape(WIDE, NO), inner)


def outer_kernel(offsets, scale, own, below, above, started, out):
    def sources(e):
        ref, first = (below, e + HALO) if e < 0 else (own, e) if e < NE else (above, e - NE)
        return ref[first * NK : (first + 1) * NK].reshape(WIDE, NO)

    mix(offsets, scale, out, sources, outer)


SMEM = pl.BlockSpec(memory_space=pltpu.SMEM)
VMEM = pl.BlockSpec(memory_space=pltpu.VMEM)
MIXED = jax.ShapeDtypeStruct((SLICES, NV, DEPTH, NO), jnp.bfloat16)


def scales(offsets, occupation, weight, table):
    return pl.pallas_call(
        weight_kernel,
        out_shape=jax.ShapeDtypeStruct((NV, 2 * WIDE, 2 * WIDE), jnp.bfloat16),
        in_specs=[SMEM] * 4,
        out_specs=VMEM,
        scratch_shapes=[pltpu.SMEM((NV, NK, NK), jnp.float32)],
    )(offsets, occupation, weight, table)


def mixed_inner(offsets, scale, own):
    return pl.pallas_call(
        inner_kernel,
        out_shape=MIXED,
        in_specs=[SMEM, VMEM, VMEM],
        out_specs=VMEM,
        compiler_params=pltpu.CompilerParams(vmem_limit_bytes=24 << 20),
    )(offsets, scale, own)


def mixed_outer(offsets, scale, own, below, above, started):
    return pl.pallas_call(
        outer_kernel,
        out_shape=MIXED,
        in_specs=[SMEM] + [VMEM] * 5,
        out_specs=VMEM,
        input_output_aliases={5: 0},
        compiler_params=pltpu.CompilerParams(vmem_limit_bytes=24 << 20),
    )(offsets, scale, own, below, above, started)


def product_kernel(coupling, shifted, out):
    for part in range(2):
        total = None
        for v in range(NV):
            block = shifted[part * 16 : part * 16 + 16, v].reshape(NO, NO)
            left = jnp.dot(coupling[v], block, preferred_element_type=jnp.float32)
            term = lax.dot_general(
                left.astype(jnp.bfloat16),
                coupling[v],
                (((1,), (1,)), ((), ())),
                preferred_element_type=jnp.float32,
            )
            total = term if total is None else total + term
        out[part] = total.astype(jnp.bfloat16)


def products(coupling, shifted):
    vmem = pl.BlockSpec(memory_space=pltpu.VMEM)
    return pl.pallas_call(
        product_kernel,
        out_shape=jax.ShapeDtypeStruct((2, NO, NO), jnp.bfloat16),
        in_specs=[vmem] * 2,
        out_specs=vmem,
        compiler_params=pltpu.CompilerParams(vmem_limit_bytes=32 << 20),
    )(coupling, shifted)


def shards(green_lesser, coupling, offsets, occupation, transfer_weight, transfer_table):
    slices = green_lesser.reshape(SLICES, DEPTH, NO)
    own = lax.all_to_all(slices, PLANE, 0, 0, tiled=True)
    half = SLICES // 2
    below = lax.ppermute(own[half:], "z", [(z, z + 1) for z in range(PLANES - 1)])
    above = lax.ppermute(own[:half], "z", [(z + 1, z) for z in range(PLANES - 1)])
    scale = scales(offsets, occupation, transfer_weight, transfer_table)
    out = mixed_outer(offsets, scale, own, below, above, mixed_inner(offsets, scale, own))
    shifted = lax.all_to_all(out.reshape(SLICES, NV * DEPTH, NO), PLANE, 0, 0, tiled=True)
    sigma = products(coupling, shifted.reshape(SLICES, NV, DEPTH, NO))
    return sigma[None, None]


def solution(mesh):
    fine = Mesh(
        mesh.devices.reshape(PLANES, ROWS, XS, HALVES, CORES),
        ("z", "lo", "x", "hi", "core"),
    )
    split = P(("z", "lo", "x"), ("hi", "core"), None, None, None)
    return jax.shard_map(
        shards,
        mesh=fine,
        in_specs=(split, P(), P(), P(), P(), P()),
        out_specs=split,
        check_vma=False,
    )
```

time: 109 us -> 106 us (0.972)
  waiting for transfers between devices: 12.6 us -> 8.33 us
    ppermute x1, waiting for transfers between devices: 9.62 us -> 5.3 us  [shards(): lax.ppermute(own[:half], 'z', [(z + 1, z) for z in range(PLANES - 1)])]
    pallas_call x1 -> x3, Pallas kernels: 4.34 us -> 5.33 us  [the longest x1 2.06 us: mixed_outer(): pl.pallas_call(outer_kernel, out_shape=MIXED, in_specs=[SMEM] + [VMEM] *...]
  transfers between devices with their start and end apart: 2 -> 2, of which waited for: 2 -> 2; matrix products, arithmetic and copies ran while one was open for 0% -> 0% of each run, Pallas kernels for 0% -> 3%
where the time goes in v2:
time: 106 us
  blocking collectives  80.4 us (76%)
  Pallas kernels  10.8 us (10%)
  waiting for transfers between devices  8.33 us (8%)
  starting transfers between devices  5.28 us (5%)
  local copies, waits for them, and re-layouts  1.12 us (1%)
    all_to_all x1, blocking collectives, shards(): lax.all_to_all(out.reshape(SLICES, NV * DEPTH, NO), PLANE, 0, 0, tiled=True)  55.3 us
    all_to_all x1, blocking collectives, shards(): own = lax.all_to_all(slices, PLANE, 0, 0, tiled=True)  25 us
    pallas_call x1, Pallas kernels, products(): pl.pallas_call(product_kernel, out_shape=jax.ShapeDtypeStruct((2, NO, NO)...  5.48 us
    ppermute x1, waiting for transfers between devices, shards(): lax.ppermute(own[:half], 'z', [(z + 1, z) for z in range(PLANES - 1)])  5.3 us
    ppermute x1, starting transfers between devices, shards(): lax.ppermute(own[half:], 'z', [(z, z + 1) for z in range(PLANES - 1)])  3.36 us
    ppermute x1, waiting for transfers between devices, shards(): lax.ppermute(own[half:], 'z', [(z, z + 1) for z in range(PLANES - 1)])  3.03 us
  transfers between devices with their start and end apart: 2, of which 2 were waited for; matrix products, arithmetic and copies ran while one was open for 0% of the time, Pallas kernels for 3%

profile of v2, /device:TPU:129, one launch (start us, length us, event | category | flops | bytes accessed | tf_op | source)
XLA Modules:
  0.0 106.0 jit_solution(5578832745034377585)
XLA Ops:
  0.0 0.0 copy-start.2
  0.0 25.0 %all_to_all.10.own = bf16[32,32,512]{2,1,0:T(8,128)(2,1)S(1)} all-to-all(bf16[32,32,512]{2,1,0:T(8,128)(2,1)} %bitcast.6), channel_id=1, replica_groups=mesh['z'=8,'lo'=2,'x'=4,'hi'=2,'core'=2] {'lo','x','hi','core'}, dimensions={0} | all-to-all | bytes 2097152 | tf_op jit(solution)/shard_map/all_to_all | solution.py:139
  25.0 0.1 fusion
  25.1 1.9 %collective-permute-start.1 = (bf16[16,32,512]{2,1,0:T(8,128)(2,1)S(1)}, bf16[16,32,512]{2,1,0:T(8,128)(2,1)S(1)}, u32[]{:S(2)}, u32[]{:S(2)}) collective-permute-start(bf16[16,32,512]{2,1,0:T(8,128)(2,1)S(1)} %get-tuple-element.5), channel_id=1, source_target_pairs={{32,0},{64,32},{96,64},{128,96},{160,128},{192,160},{224,192},{33,... | collective-permute-start | bytes 1572872 | tf_op jit(solution)/shard_map/ppermute | solution.py:142
  27.0 3.4 %collective-permute-start = (bf16[16,32,512]{2,1,0:T(8,128)(2,1)S(1)}, bf16[16,32,512]{2,1,0:T(8,128)(2,1)S(1)}, u32[]{:S(2)}, u32[]{:S(2)}) collective-permute-start(bf16[16,32,512]{2,1,0:T(8,128)(2,1)S(1)} %get-tuple-element.6), channel_id=1, source_target_pairs={{0,32},{32,64},{64,96},{96,128},{128,160},{160,192},{192,224},{1,3... | collective-permute-start | bytes 1572872 | tf_op jit(solution)/shard_map/ppermute | solution.py:141
  30.4 1.7 %shard_map.64.scale = bf16[4,256,256]{2,1,0:T(8,128)(2,1)} custom-call(s32[4]{0:T(128)} %offsets.5, f32[4]{0:T(128)} %occupation.1, f32[4,4]{1,0:T(4,128)} %weight.1, s32[4,4]{1,0:T(4,128)} %table.1), custom_call_target="tpu_custom_call" | custom-call | tf_op jit(solution)/shard_map/pallas_call | solution.py:80
  32.2 0.0 copy-done.2
  32.2 0.0 copy-start
  32.2 1.0 copy-done
  33.2 1.5 %shard_map.65.started = bf16[32,4,32,512]{3,2,1,0:T(8,128)(2,1)S(1)} custom-call(s32[4]{0:T(128)S(1)} %copy-done.2, bf16[4,256,256]{2,1,0:T(8,128)(2,1)S(1)} %copy-done, bf16[32,32,512]{2,1,0:T(8,128)(2,1)S(1)} %all_to_all.10.own), custom_call_target="tpu_custom_call" | custom-call | tf_op jit(solution)/shard_map/pallas_call | solution.py:90
  34.7 5.3 %collective-permute-done.1.above = bf16[16,32,512]{2,1,0:T(8,128)(2,1)S(1)} collective-permute-done((bf16[16,32,512]{2,1,0:T(8,128)(2,1)S(1)}, bf16[16,32,512]{2,1,0:T(8,128)(2,1)S(1)}, u32[]{:S(2)}, u32[]{:S(2)}) %collective-permute-start.1) | collective-permute-done | bytes 524320 | tf_op jit(solution)/shard_map/ppermute | solution.py:142
  40.0 3.0 %collective-permute-done.below = bf16[16,32,512]{2,1,0:T(8,128)(2,1)S(1)} collective-permute-done((bf16[16,32,512]{2,1,0:T(8,128)(2,1)S(1)}, bf16[16,32,512]{2,1,0:T(8,128)(2,1)S(1)}, u32[]{:S(2)}, u32[]{:S(2)}) %collective-permute-start) | collective-permute-done | bytes 524320 | tf_op jit(solution)/shard_map/ppermute | solution.py:141
  43.1 2.1 %shard_map.66 = bf16[32,4,32,512]{3,2,1,0:T(8,128)(2,1)S(1)} custom-call(s32[4]{0:T(128)S(1)} %copy-done.2, bf16[4,256,256]{2,1,0:T(8,128)(2,1)S(1)} %copy-done, bf16[32,32,512]{2,1,0:T(8,128)(2,1)S(1)} %all_to_all.10.own, bf16[16,32,512]{2,1,0:T(8,128)(2,1)S(1)} %collective-permute-done.below, ...), custom_call_target="tpu_custom_call", output_to_operand_aliasing={{}: (5, {})} | custom-call | tf_op jit(solution)/shard_map/pallas_call | solution.py:100
  45.1 0.0 copy-start.1
  45.1 55.3 %all_to_all.11 = bf16[32,128,512]{2,1,0:T(8,128)(2,1)S(1)} all-to-all(bf16[32,128,512]{2,1,0:T(8,128)(2,1)S(1)} %bitcast.4), channel_id=1, replica_groups=mesh['z'=8,'lo'=2,'x'=4,'hi'=2,'core'=2] {'lo','x','hi','core'}, dimensions={0} | all-to-all | bytes 8388608 | tf_op jit(solution)/shard_map/all_to_all | solution.py:145
  100.5 0.0 copy-done.1
  100.5 5.5 %shard_map.67 = bf16[2,512,512]{2,1,0:T(8,128)(2,1)} custom-call(bf16[4,512,512]{2,1,0:T(8,128)(2,1)S(1)} %copy-done.1, bf16[32,4,32,512]{3,2,1,0:T(8,128)(2,1)S(1)} %bitcast.5), custom_call_target="tpu_custom_call" | custom-call | tf_op jit(solution)/shard_map/pallas_call | solution.py:128
Async XLA Ops:
  0.0 32.2 %copy-start.2 = (s32[4]{0:T(128)S(1)}, s32[4]{0:T(128)}, u32[]{:S(2)}) copy-start(s32[4]{0:T(128)} %offsets.5) | copy-start | bytes 52
  25.1 14.9 %collective-permute-start.1 = (bf16[16,32,512]{2,1,0:T(8,128)(2,1)S(1)}, bf16[16,32,512]{2,1,0:T(8,128)(2,1)S(1)}, u32[]{:S(2)}, u32[]{:S(2)}) collective-permute-start(bf16[16,32,512]{2,1,0:T(8,128)(2,1)S(1)} %get-tuple-element.5), channel_id=1, source_target_pairs={{32,0},{64,32},{96,64},{128,96},{160,128},{192,160},{224,192},{33,... | collective-permute-start | bytes 1572872 | tf_op jit(solution)/shard_map/ppermute | solution.py:142
  27.0 16.0 %collective-permute-start = (bf16[16,32,512]{2,1,0:T(8,128)(2,1)S(1)}, bf16[16,32,512]{2,1,0:T(8,128)(2,1)S(1)}, u32[]{:S(2)}, u32[]{:S(2)}) collective-permute-start(bf16[16,32,512]{2,1,0:T(8,128)(2,1)S(1)} %get-tuple-element.6), channel_id=1, source_target_pairs={{0,32},{32,64},{64,96},{96,128},{128,160},{160,192},{192,224},{1,3... | collective-permute-start | bytes 1572872 | tf_op jit(solution)/shard_map/ppermute | solution.py:141
  32.2 1.0 copy-start
  45.1 55.3 %copy-start.1 = (bf16[4,512,512]{2,1,0:T(8,128)(2,1)S(1)}, bf16[4,512,512]{2,1,0:T(8,128)(2,1)}, u32[]{:S(2)}) copy-start(bf16[4,512,512]{2,1,0:T(8,128)(2,1)} %coupling.1) | copy-start | bytes 6291460

commit v3 on v2

--- a/solution.py
+++ b/solution.py
@@ -33,53 +33,78 @@
                 scaled = base * (occupation[v] + float(side))
                 high = scaled.astype(jnp.bfloat16)
                 rest = (scaled - high.astype(jnp.float32)).astype(jnp.bfloat16)
-                columns = slice(side * WIDE, (side + 1) * WIDE)
-                out[v, k * DEPTH : (k + 1) * DEPTH, columns] = high
-                out[v, WIDE + k * DEPTH : WIDE + (k + 1) * DEPTH, columns] = rest
+                rows = slice(k * DEPTH, (k + 1) * DEPTH)
+                out[v, rows, 2 * side * WIDE : (2 * side + 1) * WIDE] = high
+                out[v, rows, (2 * side + 1) * WIDE : (2 * side + 2) * WIDE] = rest
 
 
-def mix(offsets, scale, out, sources, energies):
-    for dist in range(1, HALO + 1):
-        mode = jnp.int32(0)
-        for v in range(1, NV):
-            mode = jnp.where(offsets[v] == dist, v, mode)
-        for e in energies(dist):
-            pair = jnp.concatenate([sources(e - dist), sources(e + dist)], axis=0)
-            total = jnp.dot(scale[mode], pair, preferred_element_type=jnp.float32)
-            total = (total[:WIDE] + total[WIDE:]).astype(jnp.bfloat16)
-            for k in range(NK):
-                out[e * NK + k, mode] = total[k * DEPTH : (k + 1) * DEPTH]
+def mode_at(offsets, dist):
+    mode = jnp.int32(0)
+    for v in range(1, NV):
+        mode = jnp.where(offsets[v] == dist, v, mode)
+    return mode
 
 
-def inner(dist):
-    return range(dist, NE - dist)
+LOW, HIGH = 0, 1
+DISTS = range(1, HALO + 1)
+PAIRS = [(dist, e) for dist in DISTS for e in range(NE)]
+BELOW = [(dist, e) for dist, e in PAIRS if e < dist]
+ABOVE = [(dist, e) for dist, e in PAIRS if e + dist >= NE]
+INNER = [pair for pair in PAIRS if pair not in BELOW + ABOVE]
 
 
-def outer(dist):
-    return [e for e in range(NE) if e not in inner(dist)]
+def block(ref, e):
+    return ref[e * NK : (e + 1) * NK].reshape(WIDE, NO)
 
 
-def inner_kernel(offsets, scale, own, out):
-    mix(offsets, scale, out, lambda e: own[e * NK : (e + 1) * NK].reshape(WIDE, NO), inner)
+def one_side(scale, mode, side, source):
+    weight = scale[mode, :, 2 * side * WIDE : (2 * side + 2) * WIDE]
+    twice = jnp.concatenate([source, source], axis=0)
+    return jnp.dot(weight, twice, preferred_element_type=jnp.float32)
 
 
-def outer_kernel(offsets, scale, own, below, above, started, out):
-    def sources(e):
-        ref, first = (below, e + HALO) if e < 0 else (own, e) if e < NE else (above, e - NE)
-        return ref[first * NK : (first + 1) * NK].reshape(WIDE, NO)
+def store(out, e, mode, total):
+    rounded = total.astype(jnp.bfloat16)
+    for k in range(NK):
+        out[e * NK + k, mode] = rounded[k * DEPTH : (k + 1) * DEPTH]
 
-    mix(offsets, scale, out, sources, outer)
+
+def inner_kernel(offsets, scale, own, out, low_rest, high_rest):
+    for dist, e in INNER:
+        mode = mode_at(offsets, dist)
+        low, high = block(own, e - dist), block(own, e + dist)
+        both = jnp.concatenate([low, low, high, high], axis=0)
+        store(out, e, mode, jnp.dot(scale[mode], both, preferred_element_type=jnp.float32))
+    for index, (dist, e) in enumerate(BELOW):
+        low_rest[index] = one_side(scale, mode_at(offsets, dist), HIGH, block(own, e + dist))
+    for index, (dist, e) in enumerate(ABOVE):
+        high_rest[index] = one_side(scale, mode_at(offsets, dist), LOW, block(own, e - dist))
+
+
+def below_kernel(offsets, scale, below, rest, started, out):
+    for index, (dist, e) in enumerate(BELOW):
+        mode = mode_at(offsets, dist)
+        term = one_side(scale, mode, LOW, block(below, e - dist + HALO))
+        store(out, e, mode, rest[index] + term)
+
+
+def above_kernel(offsets, scale, above, rest, started, out):
+    for index, (dist, e) in enumerate(ABOVE):
+        mode = mode_at(offsets, dist)
+        term = one_side(scale, mode, HIGH, block(above, e + dist - NE))
+        store(out, e, mode, rest[index] + term)
 
 
 SMEM = pl.BlockSpec(memory_space=pltpu.SMEM)
 VMEM = pl.BlockSpec(memory_space=pltpu.VMEM)
+PARAMS = pltpu.CompilerParams(vmem_limit_bytes=32 << 20)
 MIXED = jax.ShapeDtypeStruct((SLICES, NV, DEPTH, NO), jnp.bfloat16)
 
 
 def scales(offsets, occupation, weight, table):
     return pl.pallas_call(
         weight_kernel,
-        out_shape=jax.ShapeDtypeStruct((NV, 2 * WIDE, 2 * WIDE), jnp.bfloat16),
+        out_shape=jax.ShapeDtypeStruct((NV, WIDE, 4 * WIDE), jnp.bfloat16),
         in_specs=[SMEM] * 4,
         out_specs=VMEM,
         scratch_shapes=[pltpu.SMEM((NV, NK, NK), jnp.float32)],
@@ -87,24 +112,25 @@
 
 
 def mixed_inner(offsets, scale, own):
+    rests = [jax.ShapeDtypeStruct((len(p), WIDE, NO), jnp.float32) for p in (BELOW, ABOVE)]
     return pl.pallas_call(
         inner_kernel,
-        out_shape=MIXED,
+        out_shape=[MIXED, *rests],
         in_specs=[SMEM, VMEM, VMEM],
-        out_specs=VMEM,
-        compiler_params=pltpu.CompilerParams(vmem_limit_bytes=24 << 20),
+        out_specs=[VMEM] * 3,
+        compiler_params=PARAMS,
     )(offsets, scale, own)
 
 
-def mixed_outer(offsets, scale, own, below, above, started):
+def mixed_side(kernel, offsets, scale, halo, rest, started):
     return pl.pallas_call(
-        outer_kernel,
+        kernel,
         out_shape=MIXED,
-        in_specs=[SMEM] + [VMEM] * 5,
+        in_specs=[SMEM] + [VMEM] * 4,
         out_specs=VMEM,
-        input_output_aliases={5: 0},
-        compiler_params=pltpu.CompilerParams(vmem_limit_bytes=24 << 20),
-    )(offsets, scale, own, below, above, started)
+        input_output_aliases={4: 0},
+        compiler_params=PARAMS,
+    )(offsets, scale, halo, rest, started)
 
 
 def product_kernel(coupling, shifted, out):
@@ -141,7 +167,9 @@
     below = lax.ppermute(own[half:], "z", [(z, z + 1) for z in range(PLANES - 1)])
     above = lax.ppermute(own[:half], "z", [(z + 1, z) for z in range(PLANES - 1)])
     scale = scales(offsets, occupation, transfer_weight, transfer_table)
-    out = mixed_outer(offsets, scale, own, below, above, mixed_inner(offsets, scale, own))
+    out, low_rest, high_rest = mixed_inner(offsets, scale, own)
+    out = mixed_side(above_kernel, offsets, scale, above, high_rest, out)
+    out = mixed_side(below_kernel, offsets, scale, below, low_rest, out)
     shifted = lax.all_to_all(out.reshape(SLICES, NV * DEPTH, NO), PLANE, 0, 0, tiled=True)
     sigma = products(coupling, shifted.reshape(SLICES, NV, DEPTH, NO))
     return sigma[None, None]

time: 106 us -> 105 us (level)
  waiting for transfers between devices: 8.33 us -> 6.51 us
    ppermute x1, waiting for transfers between devices: 3.03 us -> 1.94 us  [shards(): lax.ppermute(own[half:], 'z', [(z, z + 1) for z in range(PLANES - 1)])]
    pallas_call x3 -> x4, Pallas kernels: 5.33 us -> 6.16 us  [the longest x1 2.24 us: mixed_inner(): pl.pallas_call(inner_kernel, out_shape=[MIXED, *rests], in_specs=[SMEM, V...]
  transfers between devices with their start and end apart: 2 -> 2, of which waited for: 2 -> 2; matrix products, arithmetic and copies ran while one was open for 0% -> 0% of each run, Pallas kernels for 3% -> 5%
where the time goes in v3:
time: 105 us
  blocking collectives  80.4 us (77%)
  Pallas kernels  11.6 us (11%)
  waiting for transfers between devices  6.51 us (6%)
  starting transfers between devices  5.28 us (5%)
  local copies, waits for them, and re-layouts  1.12 us (1%)
    all_to_all x1, blocking collectives, shards(): lax.all_to_all(out.reshape(SLICES, NV * DEPTH, NO), PLANE, 0, 0, tiled=True)  55.3 us
    all_to_all x1, blocking collectives, shards(): own = lax.all_to_all(slices, PLANE, 0, 0, tiled=True)  25 us
    pallas_call x1, Pallas kernels, products(): pl.pallas_call(product_kernel, out_shape=jax.ShapeDtypeStruct((2, NO, NO)...  5.48 us
    ppermute x1, waiting for transfers between devices, shards(): lax.ppermute(own[:half], 'z', [(z + 1, z) for z in range(PLANES - 1)])  4.58 us
    ppermute x1, starting transfers between devices, shards(): lax.ppermute(own[half:], 'z', [(z, z + 1) for z in range(PLANES - 1)])  3.36 us
    pallas_call x1, Pallas kernels, mixed_inner(): pl.pallas_call(inner_kernel, out_shape=[MIXED, *rests], in_specs=[SMEM, V...  2.24 us
    pallas_call x2, Pallas kernels, mixed_side(): pl.pallas_call(kernel, out_shape=MIXED, in_specs=[SMEM] + [VMEM] * 4, out...  2.17 us
  transfers between devices with their start and end apart: 2, of which 2 were waited for; matrix products, arithmetic and copies ran while one was open for 0% of the time, Pallas kernels for 5%

profile of v3, /device:TPU:129, one launch (start us, length us, event | category | flops | bytes accessed | tf_op | source)
XLA Modules:
  0.0 105.0 jit_solution(4531185013604303038)
XLA Ops:
  0.0 0.0 copy-start.2
  0.0 25.0 %all_to_all.10.own = bf16[32,32,512]{2,1,0:T(8,128)(2,1)S(1)} all-to-all(bf16[32,32,512]{2,1,0:T(8,128)(2,1)} %bitcast.6), channel_id=1, replica_groups=mesh['z'=8,'lo'=2,'x'=4,'hi'=2,'core'=2] {'lo','x','hi','core'}, dimensions={0} | all-to-all | bytes 2097152 | tf_op jit(solution)/shard_map/all_to_all | solution.py:165
  25.0 0.1 fusion
  25.1 1.9 %collective-permute-start.1 = (bf16[16,32,512]{2,1,0:T(8,128)(2,1)S(1)}, bf16[16,32,512]{2,1,0:T(8,128)(2,1)S(1)}, u32[]{:S(2)}, u32[]{:S(2)}) collective-permute-start(bf16[16,32,512]{2,1,0:T(8,128)(2,1)S(1)} %get-tuple-element.11), channel_id=1, source_target_pairs={{32,0},{64,32},{96,64},{128,96},{160,128},{192,160},{224,192},{33,... | collective-permute-start | bytes 1572872 | tf_op jit(solution)/shard_map/ppermute | solution.py:168
  27.0 3.4 %collective-permute-start = (bf16[16,32,512]{2,1,0:T(8,128)(2,1)S(1)}, bf16[16,32,512]{2,1,0:T(8,128)(2,1)S(1)}, u32[]{:S(2)}, u32[]{:S(2)}) collective-permute-start(bf16[16,32,512]{2,1,0:T(8,128)(2,1)S(1)} %get-tuple-element.12), channel_id=1, source_target_pairs={{0,32},{32,64},{64,96},{96,128},{128,160},{160,192},{192,224},{1,3... | collective-permute-start | bytes 1572872 | tf_op jit(solution)/shard_map/ppermute | solution.py:167
  30.4 1.7 %shard_map.64.scale = bf16[4,128,512]{2,1,0:T(8,128)(2,1)} custom-call(s32[4]{0:T(128)} %offsets.7, f32[4]{0:T(128)} %occupation.1, f32[4,4]{1,0:T(4,128)} %weight.1, s32[4,4]{1,0:T(4,128)} %table.1), custom_call_target="tpu_custom_call" | custom-call | tf_op jit(solution)/shard_map/pallas_call | solution.py:105
  32.2 0.0 copy-done.2
  32.2 0.0 copy-start
  32.2 1.0 copy-done
  33.2 2.2 %shard_map.65 = (bf16[32,4,32,512]{3,2,1,0:T(8,128)(2,1)S(1)}, f32[10,128,512]{2,1,0:T(8,128)S(1)}, f32[10,128,512]{2,1,0:T(8,128)S(1)}) custom-call(s32[4]{0:T(128)S(1)} %copy-done.2, bf16[4,128,512]{2,1,0:T(8,128)(2,1)S(1)} %copy-done, bf16[32,32,512]{2,1,0:T(8,128)(2,1)S(1)} %all_to_all.10.own), custom_call_target="tpu_custom_call" | custom-call | tf_op jit(solution)/shard_map/pallas_call | solution.py:116
  35.5 4.6 %collective-permute-done.1.above = bf16[16,32,512]{2,1,0:T(8,128)(2,1)S(1)} collective-permute-done((bf16[16,32,512]{2,1,0:T(8,128)(2,1)S(1)}, bf16[16,32,512]{2,1,0:T(8,128)(2,1)S(1)}, u32[]{:S(2)}, u32[]{:S(2)}) %collective-permute-start.1) | collective-permute-done | bytes 524320 | tf_op jit(solution)/shard_map/ppermute | solution.py:168
  40.0 1.1 %shard_map.66.started = bf16[32,4,32,512]{3,2,1,0:T(8,128)(2,1)S(1)} custom-call(s32[4]{0:T(128)S(1)} %copy-done.2, bf16[4,128,512]{2,1,0:T(8,128)(2,1)S(1)} %copy-done, bf16[16,32,512]{2,1,0:T(8,128)(2,1)S(1)} %collective-permute-done.1.above, f32[10,128,512]{2,1,0:T(8,128)S(1)} %get-tuple-element.9.rest, ...), custom_call_target="tpu_custom_call", output_to_operand_aliasing={{}: (4, {})} | custom-call | tf_op jit(solution)/shard_map/pallas_call | solution.py:126
  41.1 1.9 %collective-permute-done.below = bf16[16,32,512]{2,1,0:T(8,128)(2,1)S(1)} collective-permute-done((bf16[16,32,512]{2,1,0:T(8,128)(2,1)S(1)}, bf16[16,32,512]{2,1,0:T(8,128)(2,1)S(1)}, u32[]{:S(2)}, u32[]{:S(2)}) %collective-permute-start) | collective-permute-done | bytes 524320 | tf_op jit(solution)/shard_map/ppermute | solution.py:167
  43.1 1.1 %shard_map.67 = bf16[32,4,32,512]{3,2,1,0:T(8,128)(2,1)S(1)} custom-call(s32[4]{0:T(128)S(1)} %copy-done.2, bf16[4,128,512]{2,1,0:T(8,128)(2,1)S(1)} %copy-done, bf16[16,32,512]{2,1,0:T(8,128)(2,1)S(1)} %collective-permute-done.below, f32[10,128,512]{2,1,0:T(8,128)S(1)} %get-tuple-element.8.rest, ...), custom_call_target="tpu_custom_call", output_to_operand_aliasing={{}: (4, {})} | custom-call | tf_op jit(solution)/shard_map/pallas_call | solution.py:126
  44.1 0.0 copy-start.1
  44.2 55.3 %all_to_all.11 = bf16[32,128,512]{2,1,0:T(8,128)(2,1)S(1)} all-to-all(bf16[32,128,512]{2,1,0:T(8,128)(2,1)S(1)} %bitcast.4), channel_id=1, replica_groups=mesh['z'=8,'lo'=2,'x'=4,'hi'=2,'core'=2] {'lo','x','hi','core'}, dimensions={0} | all-to-all | bytes 8388608 | tf_op jit(solution)/shard_map/all_to_all | solution.py:173
  99.5 0.0 copy-done.1
  99.5 5.5 %shard_map.68 = bf16[2,512,512]{2,1,0:T(8,128)(2,1)} custom-call(bf16[4,512,512]{2,1,0:T(8,128)(2,1)S(1)} %copy-done.1, bf16[32,4,32,512]{3,2,1,0:T(8,128)(2,1)S(1)} %bitcast.5), custom_call_target="tpu_custom_call" | custom-call | tf_op jit(solution)/shard_map/pallas_call | solution.py:154
Async XLA Ops:
  0.0 32.2 %copy-start.2 = (s32[4]{0:T(128)S(1)}, s32[4]{0:T(128)}, u32[]{:S(2)}) copy-start(s32[4]{0:T(128)} %offsets.7) | copy-start | bytes 52
  25.1 14.9 %collective-permute-start.1 = (bf16[16,32,512]{2,1,0:T(8,128)(2,1)S(1)}, bf16[16,32,512]{2,1,0:T(8,128)(2,1)S(1)}, u32[]{:S(2)}, u32[]{:S(2)}) collective-permute-start(bf16[16,32,512]{2,1,0:T(8,128)(2,1)S(1)} %get-tuple-element.11), channel_id=1, source_target_pairs={{32,0},{64,32},{96,64},{128,96},{160,128},{192,160},{224,192},{33,... | collective-permute-start | bytes 1572872 | tf_op jit(solution)/shard_map/ppermute | solution.py:168
  27.0 16.0 %collective-permute-start = (bf16[16,32,512]{2,1,0:T(8,128)(2,1)S(1)}, bf16[16,32,512]{2,1,0:T(8,128)(2,1)S(1)}, u32[]{:S(2)}, u32[]{:S(2)}) collective-permute-start(bf16[16,32,512]{2,1,0:T(8,128)(2,1)S(1)} %get-tuple-element.12), channel_id=1, source_target_pairs={{0,32},{32,64},{64,96},{96,128},{128,160},{160,192},{192,224},{1,3... | collective-permute-start | bytes 1572872 | tf_op jit(solution)/shard_map/ppermute | solution.py:167
  32.2 1.0 copy-start
  44.1 55.3 %copy-start.1 = (bf16[4,512,512]{2,1,0:T(8,128)(2,1)S(1)}, bf16[4,512,512]{2,1,0:T(8,128)(2,1)}, u32[]{:S(2)}) copy-start(bf16[4,512,512]{2,1,0:T(8,128)(2,1)} %coupling.1) | copy-start | bytes 6291460

commit v4 on v2

v4 whole, which is shorter than its diff:
```python
import functools

import jax
import jax.numpy as jnp
from jax import lax
from jax.experimental import pallas as pl
from jax.experimental.pallas import tpu as pltpu
from jax.sharding import Mesh, PartitionSpec as P

PLANES, ROWS, XS, HALVES, CORES = 8, 2, 4, 2, 2
PLANE = ("lo", "x", "hi", "core")
NE = ROWS * XS
NK = HALVES * CORES
NV = 4
NO = 512
SLICES = NE * NK
DEPTH = 2 * NO // SLICES
HALO = 4
WIDE = NK * DEPTH


LOW, HIGH = 0, 1
DISTS = range(1, HALO + 1)


def mode_at(offsets, dist):
    mode = jnp.int32(0)
    for v in range(1, NV):
        mode = jnp.where(offsets[v] == dist, v, mode)
    return mode


def weight_kernel(offsets, occupation, weight, table, coupling, out, ordered, mixing):
    for k in range(NK):
        for q in range(NK):
            for v in range(NV):
                mixing[v, k, table[k, q]] = weight[q, v]
    row = lax.broadcasted_iota(jnp.int32, (DEPTH, WIDE), 0)
    column = lax.broadcasted_iota(jnp.int32, (DEPTH, WIDE), 1)
    for dist in DISTS:
        mode = mode_at(offsets, dist)
        ordered[dist - 1] = coupling[mode]
        for k in range(NK):
            base = jnp.zeros((DEPTH, WIDE), jnp.float32)
            for j in range(NK):
                base = jnp.where(column == row + DEPTH * j, mixing[mode, k, j], base)
            for side in (LOW, HIGH):
                scaled = base * (occupation[mode] + float(side))
                high = scaled.astype(jnp.bfloat16)
                rest = (scaled - high.astype(jnp.float32)).astype(jnp.bfloat16)
                columns = slice(side * WIDE, (side + 1) * WIDE)
                out[dist - 1, k * DEPTH : (k + 1) * DEPTH, columns] = high
                out[dist - 1, WIDE + k * DEPTH : WIDE + (k + 1) * DEPTH, columns] = rest


def block(ref, e):
    return ref[e * NK : (e + 1) * NK].reshape(WIDE, NO)


def store(out, dist, e, total):
    rounded = total.astype(jnp.bfloat16)
    for k in range(NK):
        out[e * NK + k, dist - 1] = rounded[k * DEPTH : (k + 1) * DEPTH]


def packed(dist):
    return dist * (dist - 1) // 2


def below_at(dist):
    return range(dist)


def above_at(dist):
    return range(NE - dist, NE)


def weighted(weights, source):
    total = jnp.dot(weights, source, preferred_element_type=jnp.float32)
    return total[:WIDE] + total[WIDE:]


def inner_kernel(scale, own, out, low_rest, high_rest):
    for dist in DISTS:
        weights = scale[dist - 1]
        for e in range(dist, NE - dist):
            both = jnp.concatenate([block(own, e - dist), block(own, e + dist)], axis=0)
            store(out, dist, e, weighted(weights, both))
        for index, e in enumerate(below_at(dist)):
            low_rest[packed(dist) + index] = weighted(weights[:, WIDE:], block(own, e + dist))
        for index, e in enumerate(above_at(dist)):
            high_rest[packed(dist) + index] = weighted(weights[:, :WIDE], block(own, e - dist))


def halo_kernel(side, scale, halo, rest, started, out):
    for reach in DISTS:
        source = HALO - reach if side == LOW else reach - 1
        columns = slice(side * WIDE, (side + 1) * WIDE)
        weights = scale[reach - 1 :, :, columns].reshape((HALO + 1 - reach) * 2 * WIDE, WIDE)
        total = jnp.dot(weights, block(halo, source), preferred_element_type=jnp.float32)
        for dist in range(reach, HALO + 1):
            index = dist - reach if side == LOW else reach - 1
            e = index if side == LOW else NE - dist + index
            first = (dist - reach) * 2 * WIDE
            part = total[first : first + WIDE] + total[first + WIDE : first + 2 * WIDE]
            store(out, dist, e, rest[packed(dist) + index] + part)


SMEM = pl.BlockSpec(memory_space=pltpu.SMEM)
VMEM = pl.BlockSpec(memory_space=pltpu.VMEM)
PARAMS = pltpu.CompilerParams(vmem_limit_bytes=18 << 20)
MIXED = jax.ShapeDtypeStruct((SLICES, NV, DEPTH, NO), jnp.bfloat16)
REST = jax.ShapeDtypeStruct((HALO * (HALO + 1) // 2, WIDE, NO), jnp.float32)


def by_distance(offsets, occupation, weight, table, coupling):
    return pl.pallas_call(
        weight_kernel,
        out_shape=[
            jax.ShapeDtypeStruct((HALO, 2 * WIDE, 2 * WIDE), jnp.bfloat16),
            jax.ShapeDtypeStruct((HALO, NO, NO), jnp.bfloat16),
        ],
        in_specs=[SMEM] * 4 + [VMEM],
        out_specs=[VMEM] * 2,
        scratch_shapes=[pltpu.SMEM((NV, NK, NK), jnp.float32)],
        compiler_params=PARAMS,
    )(offsets, occupation, weight, table, coupling)


def mixed_inner(scale, own):
    return pl.pallas_call(
        inner_kernel,
        out_shape=[MIXED, REST, REST],
        in_specs=[VMEM] * 2,
        out_specs=[VMEM] * 3,
        compiler_params=PARAMS,
    )(scale, own)


def mixed_side(side, scale, halo, rest, started):
    return pl.pallas_call(
        functools.partial(halo_kernel, side),
        out_shape=MIXED,
        in_specs=[VMEM] * 4,
        out_specs=VMEM,
        input_output_aliases={3: 0},
        compiler_params=PARAMS,
    )(scale, halo, rest, started)


def product_kernel(coupling, shifted, out):
    for part in range(2):
        total = None
        for v in range(NV):
            block = shifted[part * 16 : part * 16 + 16, v].reshape(NO, NO)
            left = jnp.dot(coupling[v], block, preferred_element_type=jnp.float32)
            term = lax.dot_general(
                left.astype(jnp.bfloat16),
                coupling[v],
                (((1,), (1,)), ((), ())),
                preferred_element_type=jnp.float32,
            )
            total = term if total is None else total + term
        out[part] = total.astype(jnp.bfloat16)


def products(coupling, shifted):
    vmem = pl.BlockSpec(memory_space=pltpu.VMEM)
    return pl.pallas_call(
        product_kernel,
        out_shape=jax.ShapeDtypeStruct((2, NO, NO), jnp.bfloat16),
        in_specs=[vmem] * 2,
        out_specs=vmem,
        compiler_params=pltpu.CompilerParams(vmem_limit_bytes=18 << 20),
    )(coupling, shifted)


def shards(green_lesser, coupling, offsets, occupation, transfer_weight, transfer_table):
    slices = green_lesser.reshape(SLICES, DEPTH, NO)
    own = lax.all_to_all(slices, PLANE, 0, 0, tiled=True)
    half = SLICES // 2
    below = lax.ppermute(own[half:], "z", [(z, z + 1) for z in range(PLANES - 1)])
    above = lax.ppermute(own[:half], "z", [(z + 1, z) for z in range(PLANES - 1)])
    scale, ordered = by_distance(offsets, occupation, transfer_weight, transfer_table, coupling)
    out, low_rest, high_rest = mixed_inner(scale, own)
    out = mixed_side(HIGH, scale, above, high_rest, out)
    out = mixed_side(LOW, scale, below, low_rest, out)
    shifted = lax.all_to_all(out.reshape(SLICES, NV * DEPTH, NO), PLANE, 0, 0, tiled=True)
    sigma = products(ordered, shifted.reshape(SLICES, NV, DEPTH, NO))
    return sigma[None, None]


def solution(mesh):
    fine = Mesh(
        mesh.devices.reshape(PLANES, ROWS, XS, HALVES, CORES),
        ("z", "lo", "x", "hi", "core"),
    )
    split = P(("z", "lo", "x"), ("hi", "core"), None, None, None)
    return jax.shard_map(
        shards,
        mesh=fine,
        in_specs=(split, P(), P(), P(), P(), P()),
        out_specs=split,
        check_vma=False,
    )
```

time: 106 us -> 105 us (level)
    pallas_call x3 -> x4, Pallas kernels: 5.33 us -> 4.88 us  [the longest x1 2.34 us: mixed_inner(): pl.pallas_call(inner_kernel, out_shape=[MIXED, REST, REST], in_specs=[VME...]
  transfers between devices with their start and end apart: 2 -> 2, of which waited for: 2 -> 2; matrix products, arithmetic and copies ran while one was open for 0% -> 0% of each run, Pallas kernels for 3% -> 4%
where the time goes in v4:
time: 105 us
  blocking collectives  80.2 us (76%)
  Pallas kernels  10.4 us (10%)
  waiting for transfers between devices  8.52 us (8%)
  starting transfers between devices  5.28 us (5%)
    all_to_all x1, blocking collectives, shards(): lax.all_to_all(out.reshape(SLICES, NV * DEPTH, NO), PLANE, 0, 0, tiled=True)  55.2 us
    all_to_all x1, blocking collectives, shards(): own = lax.all_to_all(slices, PLANE, 0, 0, tiled=True)  25.1 us
    ppermute x1, waiting for transfers between devices, shards(): lax.ppermute(own[:half], 'z', [(z + 1, z) for z in range(PLANES - 1)])  6.32 us
    pallas_call x1, Pallas kernels, products(): pl.pallas_call(product_kernel, out_shape=jax.ShapeDtypeStruct((2, NO, NO)...  5.48 us
    ppermute x1, starting transfers between devices, shards(): lax.ppermute(own[half:], 'z', [(z, z + 1) for z in range(PLANES - 1)])  3.36 us
    pallas_call x1, Pallas kernels, mixed_inner(): pl.pallas_call(inner_kernel, out_shape=[MIXED, REST, REST], in_specs=[VME...  2.34 us
    ppermute x1, waiting for transfers between devices, shards(): lax.ppermute(own[half:], 'z', [(z, z + 1) for z in range(PLANES - 1)])  2.2 us
  transfers between devices with their start and end apart: 2, of which 2 were waited for; matrix products, arithmetic and copies ran while one was open for 0% of the time, Pallas kernels for 4%

profile of v4, /device:TPU:129, one launch (start us, length us, event | category | flops | bytes accessed | tf_op | source)
XLA Modules:
  0.0 104.6 jit_solution(4272763205896748538)
XLA Ops:
  0.0 0.0 copy-start.2
  0.0 0.0 copy-start.1
  0.0 0.0 copy-start.4
  0.0 0.0 copy-start.3
  0.0 0.0 copy-start
  0.0 25.1 %all_to_all.10.own = bf16[32,32,512]{2,1,0:T(8,128)(2,1)S(1)} all-to-all(bf16[32,32,512]{2,1,0:T(8,128)(2,1)} %bitcast.6), channel_id=1, replica_groups=mesh['z'=8,'lo'=2,'x'=4,'hi'=2,'core'=2] {'lo','x','hi','core'}, dimensions={0} | all-to-all | bytes 2097152 | tf_op jit(solution)/shard_map/all_to_all | solution.py:180
  25.1 0.1 fusion
  25.2 1.9 %collective-permute-start.1 = (bf16[16,32,512]{2,1,0:T(8,128)(2,1)S(1)}, bf16[16,32,512]{2,1,0:T(8,128)(2,1)S(1)}, u32[]{:S(2)}, u32[]{:S(2)}) collective-permute-start(bf16[16,32,512]{2,1,0:T(8,128)(2,1)S(1)} %get-tuple-element.15), channel_id=1, source_target_pairs={{32,0},{64,32},{96,64},{128,96},{160,128},{192,160},{224,192},{33,... | collective-permute-start | bytes 1572872 | tf_op jit(solution)/shard_map/ppermute | solution.py:183
  27.1 3.4 %collective-permute-start = (bf16[16,32,512]{2,1,0:T(8,128)(2,1)S(1)}, bf16[16,32,512]{2,1,0:T(8,128)(2,1)S(1)}, u32[]{:S(2)}, u32[]{:S(2)}) collective-permute-start(bf16[16,32,512]{2,1,0:T(8,128)(2,1)S(1)} %get-tuple-element.16), channel_id=1, source_target_pairs={{0,32},{32,64},{64,96},{96,128},{128,160},{160,192},{192,224},{1,3... | collective-permute-start | bytes 1572872 | tf_op jit(solution)/shard_map/ppermute | solution.py:182
  30.5 0.0 copy-done.2
  30.5 0.0 copy-done.1
  30.5 0.0 copy-done.4
  30.5 0.0 copy-done.3
  30.5 0.0 copy-done
  30.5 0.9 shard_map.64
  31.4 2.3 %shard_map.65 = (bf16[32,4,32,512]{3,2,1,0:T(8,128)(2,1)S(1)}, f32[10,128,512]{2,1,0:T(8,128)S(1)}, f32[10,128,512]{2,1,0:T(8,128)S(1)}) custom-call(bf16[4,256,256]{2,1,0:T(8,128)(2,1)S(1)} %get-tuple-element.11.scale, bf16[32,32,512]{2,1,0:T(8,128)(2,1)S(1)} %all_to_all.10.own), custom_call_target="tpu_custom_call" | custom-call | tf_op jit(solution)/shard_map/pallas_call | solution.py:131
  33.8 6.3 %collective-permute-done.1.halo = bf16[16,32,512]{2,1,0:T(8,128)(2,1)S(1)} collective-permute-done((bf16[16,32,512]{2,1,0:T(8,128)(2,1)S(1)}, bf16[16,32,512]{2,1,0:T(8,128)(2,1)S(1)}, u32[]{:S(2)}, u32[]{:S(2)}) %collective-permute-start.1) | collective-permute-done | bytes 524320 | tf_op jit(solution)/shard_map/ppermute | solution.py:183
  40.1 0.8 shard_map.66.started
  40.9 2.2 %collective-permute-done.halo = bf16[16,32,512]{2,1,0:T(8,128)(2,1)S(1)} collective-permute-done((bf16[16,32,512]{2,1,0:T(8,128)(2,1)S(1)}, bf16[16,32,512]{2,1,0:T(8,128)(2,1)S(1)}, u32[]{:S(2)}, u32[]{:S(2)}) %collective-permute-start) | collective-permute-done | bytes 524320 | tf_op jit(solution)/shard_map/ppermute | solution.py:182
  43.1 0.8 shard_map.67
  43.9 55.2 %all_to_all.11 = bf16[32,128,512]{2,1,0:T(8,128)(2,1)S(1)} all-to-all(bf16[32,128,512]{2,1,0:T(8,128)(2,1)S(1)} %bitcast.4), channel_id=1, replica_groups=mesh['z'=8,'lo'=2,'x'=4,'hi'=2,'core'=2] {'lo','x','hi','core'}, dimensions={0} | all-to-all | bytes 8388608 | tf_op jit(solution)/shard_map/all_to_all | solution.py:188
  99.1 5.5 %shard_map.68 = bf16[2,512,512]{2,1,0:T(8,128)(2,1)} custom-call(bf16[4,512,512]{2,1,0:T(8,128)(2,1)S(1)} %get-tuple-element.10.coupling, bf16[32,4,32,512]{3,2,1,0:T(8,128)(2,1)S(1)} %bitcast.5), custom_call_target="tpu_custom_call" | custom-call | tf_op jit(solution)/shard_map/pallas_call | solution.py:169
Async XLA Ops:
  0.0 30.5 %copy-start.2 = (s32[4,4]{1,0:T(4,128)S(1)}, s32[4,4]{1,0:T(4,128)}, u32[]{:S(2)}) copy-start(s32[4,4]{1,0:T(4,128)} %table.1) | copy-start | bytes 196
  0.0 30.5 %copy-start.1 = (f32[4,4]{1,0:T(4,128)S(1)}, f32[4,4]{1,0:T(4,128)}, u32[]{:S(2)}) copy-start(f32[4,4]{1,0:T(4,128)} %weight.1) | copy-start | bytes 196
  0.0 30.5 %copy-start.4 = (f32[4]{0:T(128)S(1)}, f32[4]{0:T(128)}, u32[]{:S(2)}) copy-start(f32[4]{0:T(128)} %occupation.1) | copy-start | bytes 52
  0.0 30.5 %copy-start.3 = (s32[4]{0:T(128)S(1)}, s32[4]{0:T(128)}, u32[]{:S(2)}) copy-start(s32[4]{0:T(128)} %offsets.1) | copy-start | bytes 52
  0.0 30.5 %copy-start = (bf16[4,512,512]{2,1,0:T(8,128)(2,1)S(1)}, bf16[4,512,512]{2,1,0:T(8,128)(2,1)}, u32[]{:S(2)}) copy-start(bf16[4,512,512]{2,1,0:T(8,128)(2,1)} %coupling.1) | copy-start | bytes 6291460
  25.2 14.9 %collective-permute-start.1 = (bf16[16,32,512]{2,1,0:T(8,128)(2,1)S(1)}, bf16[16,32,512]{2,1,0:T(8,128)(2,1)S(1)}, u32[]{:S(2)}, u32[]{:S(2)}) collective-permute-start(bf16[16,32,512]{2,1,0:T(8,128)(2,1)S(1)} %get-tuple-element.15), channel_id=1, source_target_pairs={{32,0},{64,32},{96,64},{128,96},{160,128},{192,160},{224,192},{33,... | collective-permute-start | bytes 1572872 | tf_op jit(solution)/shard_map/ppermute | solution.py:183
  27.1 16.0 %collective-permute-start = (bf16[16,32,512]{2,1,0:T(8,128)(2,1)S(1)}, bf16[16,32,512]{2,1,0:T(8,128)(2,1)S(1)}, u32[]{:S(2)}, u32[]{:S(2)}) collective-permute-start(bf16[16,32,512]{2,1,0:T(8,128)(2,1)S(1)} %get-tuple-element.16), channel_id=1, source_target_pairs={{0,32},{32,64},{64,96},{96,128},{128,160},{160,192},{192,224},{1,3... | collective-permute-start | bytes 1572872 | tf_op jit(solution)/shard_map/ppermute | solution.py:182

commit v5 on v4

--- a/solution.py
+++ b/solution.py
@@ -30,7 +30,7 @@
     return mode
 
 
-def weight_kernel(offsets, occupation, weight, table, coupling, out, ordered, mixing):
+def weight_kernel(offsets, occupation, weight, table, coupling, out, ordered, turned, mixing):
     for k in range(NK):
         for q in range(NK):
             for v in range(NV):
@@ -40,6 +40,7 @@
     for dist in DISTS:
         mode = mode_at(offsets, dist)
         ordered[dist - 1] = coupling[mode]
+        turned[dist - 1] = coupling[mode].T
         for k in range(NK):
             base = jnp.zeros((DEPTH, WIDE), jnp.float32)
             for j in range(NK):
@@ -57,10 +58,13 @@
     return ref[e * NK : (e + 1) * NK].reshape(WIDE, NO)
 
 
-def store(out, dist, e, total):
-    rounded = total.astype(jnp.bfloat16)
-    for k in range(NK):
-        out[e * NK + k, dist - 1] = rounded[k * DEPTH : (k + 1) * DEPTH]
+def times_right(turned, dist, rows, energies, out):
+    right = jnp.dot(rows, turned[dist - 1], preferred_element_type=jnp.float32)
+    right = right.astype(jnp.bfloat16)
+    for index, e in enumerate(energies):
+        for k in range(NK):
+            first = index * WIDE + k * DEPTH
+            out[e * NK + k, dist - 1] = right[first : first + DEPTH]
 
 
 def packed(dist):
@@ -80,30 +84,37 @@
     return total[:WIDE] + total[WIDE:]
 
 
-def inner_kernel(scale, own, out, low_rest, high_rest):
+def inner_kernel(scale, turned, own, out, low_rest, high_rest, sums):
     for dist in DISTS:
         weights = scale[dist - 1]
-        for e in range(dist, NE - dist):
+        energies = range(dist, NE - dist)
+        for index, e in enumerate(energies):
             both = jnp.concatenate([block(own, e - dist), block(own, e + dist)], axis=0)
-            store(out, dist, e, weighted(weights, both))
+            sums[index] = weighted(weights, both).astype(jnp.bfloat16)
+        if energies:
+            rows = sums[0 : len(energies)].reshape(len(energies) * WIDE, NO)
+            times_right(turned, dist, rows, energies, out)
         for index, e in enumerate(below_at(dist)):
             low_rest[packed(dist) + index] = weighted(weights[:, WIDE:], block(own, e + dist))
         for index, e in enumerate(above_at(dist)):
             high_rest[packed(dist) + index] = weighted(weights[:, :WIDE], block(own, e - dist))
 
 
-def halo_kernel(side, scale, halo, rest, started, out):
+def halo_kernel(side, scale, turned, halo, rest, started, out, sums):
     for reach in DISTS:
         source = HALO - reach if side == LOW else reach - 1
         columns = slice(side * WIDE, (side + 1) * WIDE)
         weights = scale[reach - 1 :, :, columns].reshape((HALO + 1 - reach) * 2 * WIDE, WIDE)
         total = jnp.dot(weights, block(halo, source), preferred_element_type=jnp.float32)
         for dist in range(reach, HALO + 1):
-            index = dist - reach if side == LOW else reach - 1
-            e = index if side == LOW else NE - dist + index
+            index = packed(dist) + (dist - reach if side == LOW else reach - 1)
             first = (dist - reach) * 2 * WIDE
             part = total[first : first + WIDE] + total[first + WIDE : first + 2 * WIDE]
-            store(out, dist, e, rest[packed(dist) + index] + part)
+            sums[index] = (rest[index] + part).astype(jnp.bfloat16)
+    for dist in DISTS:
+        rows = sums[packed(dist) : packed(dist) + dist].reshape(dist * WIDE, NO)
+        energies = below_at(dist) if side == LOW else above_at(dist)
+        times_right(turned, dist, rows, energies, out)
 
 
 SMEM = pl.BlockSpec(memory_space=pltpu.SMEM)
@@ -119,47 +130,45 @@
         out_shape=[
             jax.ShapeDtypeStruct((HALO, 2 * WIDE, 2 * WIDE), jnp.bfloat16),
             jax.ShapeDtypeStruct((HALO, NO, NO), jnp.bfloat16),
+            jax.ShapeDtypeStruct((HALO, NO, NO), jnp.bfloat16),
         ],
         in_specs=[SMEM] * 4 + [VMEM],
-        out_specs=[VMEM] * 2,
+        out_specs=[VMEM] * 3,
         scratch_shapes=[pltpu.SMEM((NV, NK, NK), jnp.float32)],
         compiler_params=PARAMS,
     )(offsets, occupation, weight, table, coupling)
 
 
-def mixed_inner(scale, own):
+def mixed_inner(scale, turned, own):
     return pl.pallas_call(
         inner_kernel,
         out_shape=[MIXED, REST, REST],
-        in_specs=[VMEM] * 2,
+        in_specs=[VMEM] * 3,
         out_specs=[VMEM] * 3,
+        scratch_shapes=[pltpu.VMEM((NE, WIDE, NO), jnp.bfloat16)],
         compiler_params=PARAMS,
-    )(scale, own)
-
-
-def mixed_side(side, scale, halo, rest, started):
+    )(scale, turned, own)
+
+
+def mixed_side(side, scale, turned, halo, rest, started):
     return pl.pallas_call(
         functools.partial(halo_kernel, side),
         out_shape=MIXED,
-        in_specs=[VMEM] * 4,
+        in_specs=[VMEM] * 5,
         out_specs=VMEM,
-        input_output_aliases={3: 0},
+        input_output_aliases={4: 0},
+        scratch_shapes=[pltpu.VMEM(REST.shape, jnp.bfloat16)],
         compiler_params=PARAMS,
-    )(scale, halo, rest, started)
-
-
-def product_kernel(coupling, shifted, out):
+    )(scale, turned, halo, rest, started)
+
+
+def product_kernel(ordered, right, out):
+    half = SLICES // 2
     for part in range(2):
         total = None
-        for v in range(NV):
-            block = shifted[part * 16 : part * 16 + 16, v].reshape(NO, NO)
-            left = jnp.dot(coupling[v], block, preferred_element_type=jnp.float32)
-            term = lax.dot_general(
-                left.astype(jnp.bfloat16),
-                coupling[v],
-                (((1,), (1,)), ((), ())),
-                preferred_element_type=jnp.float32,
-            )
+        for index in range(HALO):
+            rows = right[part * half : part * half + half, index].reshape(NO, NO)
+            term = jnp.dot(ordered[index], rows, preferred_element_type=jnp.float32)
             total = term if total is None else total + term
         out[part] = total.astype(jnp.bfloat16)
 
@@ -181,10 +190,10 @@
     half = SLICES // 2
     below = lax.ppermute(own[half:], "z", [(z, z + 1) for z in range(PLANES - 1)])
     above = lax.ppermute(own[:half], "z", [(z + 1, z) for z in range(PLANES - 1)])
-    scale, ordered = by_distance(offsets, occupation, transfer_weight, transfer_table, coupling)
-    out, low_rest, high_rest = mixed_inner(scale, own)
-    out = mixed_side(HIGH, scale, above, high_rest, out)
-    out = mixed_side(LOW, scale, below, low_rest, out)
+    scale, ordered, turned = by_distance(offsets, occupation, transfer_weight, transfer_table, coupling)
+    out, low_rest, high_rest = mixed_inner(scale, turned, own)
+    out = mixed_side(HIGH, scale, turned, above, high_rest, out)
+    out = mixed_side(LOW, scale, turned, below, low_rest, out)
     shifted = lax.all_to_all(out.reshape(SLICES, NV * DEPTH, NO), PLANE, 0, 0, tiled=True)
     sigma = products(ordered, shifted.reshape(SLICES, NV, DEPTH, NO))
     return sigma[None, None]

time: 105 us -> 103 us (0.981)
  waiting for transfers between devices: 8.52 us -> 6.54 us
    pallas_call x1, Pallas kernels: 5.48 us -> 3.3 us  [products(): pl.pallas_call(product_kernel, out_shape=jax.ShapeDtypeStruct((2, NO, NO)...]
    pallas_call x2, Pallas kernels: 1.64 us -> 3.01 us  [mixed_side(): pl.pallas_call(functools.partial(halo_kernel, side), out_shape=MIXED, in_...]
    ppermute x1, waiting for transfers between devices: 6.32 us -> 5.02 us  [shards(): lax.ppermute(own[:half], 'z', [(z + 1, z) for z in range(PLANES - 1)])]
  transfers between devices with their start and end apart: 2 -> 2, of which waited for: 2 -> 2; matrix products, arithmetic and copies ran while one was open for 0% -> 0% of each run, Pallas kernels for 4% -> 6%
where the time goes in v5:
time: 103 us
  blocking collectives  80.2 us (78%)
  Pallas kernels  10.8 us (10%)
  waiting for transfers between devices  6.54 us (6%)
  starting transfers between devices  5.28 us (5%)
    all_to_all x1, blocking collectives, shards(): lax.all_to_all(out.reshape(SLICES, NV * DEPTH, NO), PLANE, 0, 0, tiled=True)  55.2 us
    all_to_all x1, blocking collectives, shards(): own = lax.all_to_all(slices, PLANE, 0, 0, tiled=True)  25.1 us
    ppermute x1, waiting for transfers between devices, shards(): lax.ppermute(own[:half], 'z', [(z + 1, z) for z in range(PLANES - 1)])  5.02 us
    ppermute x1, starting transfers between devices, shards(): lax.ppermute(own[half:], 'z', [(z, z + 1) for z in range(PLANES - 1)])  3.36 us
    pallas_call x1, Pallas kernels, products(): pl.pallas_call(product_kernel, out_shape=jax.ShapeDtypeStruct((2, NO, NO)...  3.3 us
    pallas_call x1, Pallas kernels, mixed_inner(): pl.pallas_call(inner_kernel, out_shape=[MIXED, REST, REST], in_specs=[VME...  3.22 us
    pallas_call x2, Pallas kernels, mixed_side(): pl.pallas_call(functools.partial(halo_kernel, side), out_shape=MIXED, in_...  3.01 us
  transfers between devices with their start and end apart: 2, of which 2 were waited for; matrix products, arithmetic and copies ran while one was open for 0% of the time, Pallas kernels for 6%

profile of v5, /device:TPU:129, one launch (start us, length us, event | category | flops | bytes accessed | tf_op | source)
XLA Modules:
  0.0 103.1 jit_solution(15578384872541919626)
XLA Ops:
  0.0 0.0 copy-start.2
  0.0 0.0 copy-start.1
  0.0 0.0 copy-start.4
  0.0 0.0 copy-start.3
  0.0 0.0 copy-start
  0.0 25.1 %all_to_all.10.own = bf16[32,32,512]{2,1,0:T(8,128)(2,1)S(1)} all-to-all(bf16[32,32,512]{2,1,0:T(8,128)(2,1)} %bitcast.6), channel_id=1, replica_groups=mesh['z'=8,'lo'=2,'x'=4,'hi'=2,'core'=2] {'lo','x','hi','core'}, dimensions={0} | all-to-all | bytes 2097152 | tf_op jit(solution)/shard_map/all_to_all | solution.py:189
  25.1 0.1 fusion
  25.2 1.9 %collective-permute-start.1 = (bf16[16,32,512]{2,1,0:T(8,128)(2,1)S(1)}, bf16[16,32,512]{2,1,0:T(8,128)(2,1)S(1)}, u32[]{:S(2)}, u32[]{:S(2)}) collective-permute-start(bf16[16,32,512]{2,1,0:T(8,128)(2,1)S(1)} %get-tuple-element.17), channel_id=1, source_target_pairs={{32,0},{64,32},{96,64},{128,96},{160,128},{192,160},{224,192},{33,... | collective-permute-start | bytes 1572872 | tf_op jit(solution)/shard_map/ppermute | solution.py:192
  27.1 3.4 %collective-permute-start = (bf16[16,32,512]{2,1,0:T(8,128)(2,1)S(1)}, bf16[16,32,512]{2,1,0:T(8,128)(2,1)S(1)}, u32[]{:S(2)}, u32[]{:S(2)}) collective-permute-start(bf16[16,32,512]{2,1,0:T(8,128)(2,1)S(1)} %get-tuple-element.18), channel_id=1, source_target_pairs={{0,32},{32,64},{64,96},{96,128},{128,160},{160,192},{192,224},{1,3... | collective-permute-start | bytes 1572872 | tf_op jit(solution)/shard_map/ppermute | solution.py:191
  30.5 0.0 copy-done.2
  30.5 0.0 copy-done.1
  30.5 0.0 copy-done.4
  30.5 0.0 copy-done.3
  30.5 0.0 copy-done
  30.5 1.3 %shard_map.64 = (bf16[4,256,256]{2,1,0:T(8,128)(2,1)S(1)}, bf16[4,512,512]{2,1,0:T(8,128)(2,1)S(1)}, bf16[4,512,512]{2,1,0:T(8,128)(2,1)S(1)}) custom-call(s32[4]{0:T(128)S(1)} %copy-done.3, f32[4]{0:T(128)S(1)} %copy-done.4, f32[4,4]{1,0:T(4,128)S(1)} %copy-done.1, s32[4,4]{1,0:T(4,128)S(1)} %copy-done.2, bf16[4,512,512]{2,1,0:T(8,128)(2,1)S(1)} %copy-done), custom_call_target="tpu_custom_call" | custom-call | tf_op jit(solution)/shard_map/pallas_call | solution.py:128
  31.8 3.2 %shard_map.65 = (bf16[32,4,32,512]{3,2,1,0:T(8,128)(2,1)S(1)}, f32[10,128,512]{2,1,0:T(8,128)S(1)}, f32[10,128,512]{2,1,0:T(8,128)S(1)}) custom-call(bf16[4,256,256]{2,1,0:T(8,128)(2,1)S(1)} %get-tuple-element.12.scale, bf16[4,512,512]{2,1,0:T(8,128)(2,1)S(1)} %get-tuple-element.13.turned, bf16[32,32,512]{2,1,0:T(8,128)(2,1)S(1)} %all_to_all.10.own), custom_call_target="tpu_custom_call" | custom-call | tf_op jit(solution)/shard_map/pallas_call | solution.py:143
  35.1 5.0 %collective-permute-done.1.halo = bf16[16,32,512]{2,1,0:T(8,128)(2,1)S(1)} collective-permute-done((bf16[16,32,512]{2,1,0:T(8,128)(2,1)S(1)}, bf16[16,32,512]{2,1,0:T(8,128)(2,1)S(1)}, u32[]{:S(2)}, u32[]{:S(2)}) %collective-permute-start.1) | collective-permute-done | bytes 524320 | tf_op jit(solution)/shard_map/ppermute | solution.py:192
  40.1 1.5 %shard_map.66.started = bf16[32,4,32,512]{3,2,1,0:T(8,128)(2,1)S(1)} custom-call(bf16[4,256,256]{2,1,0:T(8,128)(2,1)S(1)} %get-tuple-element.12.scale, bf16[4,512,512]{2,1,0:T(8,128)(2,1)S(1)} %get-tuple-element.13.turned, bf16[16,32,512]{2,1,0:T(8,128)(2,1)S(1)} %collective-permute-done.1.halo, ...), custom_call_target="tpu_custom_call", output_to_operand_aliasing={{}: (4, {})} | custom-call | tf_op jit(solution)/shard_map/pallas_call | solution.py:154
  41.6 1.5 %collective-permute-done.halo = bf16[16,32,512]{2,1,0:T(8,128)(2,1)S(1)} collective-permute-done((bf16[16,32,512]{2,1,0:T(8,128)(2,1)S(1)}, bf16[16,32,512]{2,1,0:T(8,128)(2,1)S(1)}, u32[]{:S(2)}, u32[]{:S(2)}) %collective-permute-start) | collective-permute-done | bytes 524320 | tf_op jit(solution)/shard_map/ppermute | solution.py:191
  43.1 1.5 %shard_map.67 = bf16[32,4,32,512]{3,2,1,0:T(8,128)(2,1)S(1)} custom-call(bf16[4,256,256]{2,1,0:T(8,128)(2,1)S(1)} %get-tuple-element.12.scale, bf16[4,512,512]{2,1,0:T(8,128)(2,1)S(1)} %get-tuple-element.13.turned, bf16[16,32,512]{2,1,0:T(8,128)(2,1)S(1)} %collective-permute-done.halo, ...), custom_call_target="tpu_custom_call", output_to_operand_aliasing={{}: (4, {})} | custom-call | tf_op jit(solution)/shard_map/pallas_call | solution.py:154
  44.6 55.2 %all_to_all.11 = bf16[32,128,512]{2,1,0:T(8,128)(2,1)S(1)} all-to-all(bf16[32,128,512]{2,1,0:T(8,128)(2,1)S(1)} %bitcast.4), channel_id=1, replica_groups=mesh['z'=8,'lo'=2,'x'=4,'hi'=2,'core'=2] {'lo','x','hi','core'}, dimensions={0} | all-to-all | bytes 8388608 | tf_op jit(solution)/shard_map/all_to_all | solution.py:197
  99.8 3.3 %shard_map.68 = bf16[2,512,512]{2,1,0:T(8,128)(2,1)} custom-call(bf16[4,512,512]{2,1,0:T(8,128)(2,1)S(1)} %get-tuple-element.11.ordered, bf16[32,4,32,512]{3,2,1,0:T(8,128)(2,1)S(1)} %bitcast.5), custom_call_target="tpu_custom_call" | custom-call | tf_op jit(solution)/shard_map/pallas_call | solution.py:178
Async XLA Ops:
  0.0 30.5 %copy-start.2 = (s32[4,4]{1,0:T(4,128)S(1)}, s32[4,4]{1,0:T(4,128)}, u32[]{:S(2)}) copy-start(s32[4,4]{1,0:T(4,128)} %table.1) | copy-start | bytes 196
  0.0 30.5 %copy-start.1 = (f32[4,4]{1,0:T(4,128)S(1)}, f32[4,4]{1,0:T(4,128)}, u32[]{:S(2)}) copy-start(f32[4,4]{1,0:T(4,128)} %weight.1) | copy-start | bytes 196
  0.0 30.5 %copy-start.4 = (f32[4]{0:T(128)S(1)}, f32[4]{0:T(128)}, u32[]{:S(2)}) copy-start(f32[4]{0:T(128)} %occupation.1) | copy-start | bytes 52
  0.0 30.5 %copy-start.3 = (s32[4]{0:T(128)S(1)}, s32[4]{0:T(128)}, u32[]{:S(2)}) copy-start(s32[4]{0:T(128)} %offsets.1) | copy-start | bytes 52
  0.0 30.5 %copy-start = (bf16[4,512,512]{2,1,0:T(8,128)(2,1)S(1)}, bf16[4,512,512]{2,1,0:T(8,128)(2,1)}, u32[]{:S(2)}) copy-start(bf16[4,512,512]{2,1,0:T(8,128)(2,1)} %coupling.1) | copy-start | bytes 6291460
  25.2 14.9 %collective-permute-start.1 = (bf16[16,32,512]{2,1,0:T(8,128)(2,1)S(1)}, bf16[16,32,512]{2,1,0:T(8,128)(2,1)S(1)}, u32[]{:S(2)}, u32[]{:S(2)}) collective-permute-start(bf16[16,32,512]{2,1,0:T(8,128)(2,1)S(1)} %get-tuple-element.17), channel_id=1, source_target_pairs={{32,0},{64,32},{96,64},{128,96},{160,128},{192,160},{224,192},{33,... | collective-permute-start | bytes 1572872 | tf_op jit(solution)/shard_map/ppermute | solution.py:192
  27.1 16.0 %collective-permute-start = (bf16[16,32,512]{2,1,0:T(8,128)(2,1)S(1)}, bf16[16,32,512]{2,1,0:T(8,128)(2,1)S(1)}, u32[]{:S(2)}, u32[]{:S(2)}) collective-permute-start(bf16[16,32,512]{2,1,0:T(8,128)(2,1)S(1)} %get-tuple-element.18), channel_id=1, source_target_pairs={{0,32},{32,64},{64,96},{96,128},{128,160},{160,192},{192,224},{1,3... | collective-permute-start | bytes 1572872 | tf_op jit(solution)/shard_map/ppermute | solution.py:191

commit v6 on v5

--- a/solution.py
+++ b/solution.py
@@ -162,26 +162,35 @@
     )(scale, turned, halo, rest, started)
 
 
-def product_kernel(ordered, right, out):
+def product_kernel(ordered, right, out, ready, sems):
     half = SLICES // 2
+    copies = []
     for part in range(2):
         total = None
         for index in range(HALO):
             rows = right[part * half : part * half + half, index].reshape(NO, NO)
             term = jnp.dot(ordered[index], rows, preferred_element_type=jnp.float32)
             total = term if total is None else total + term
-        out[part] = total.astype(jnp.bfloat16)
-
-
-def products(coupling, shifted):
-    vmem = pl.BlockSpec(memory_space=pltpu.VMEM)
+        ready[part] = total.astype(jnp.bfloat16)
+        copy = pltpu.make_async_copy(ready.at[part], out.at[part], sems.at[part])
+        copy.start()
+        copies.append(copy)
+    for copy in copies:
+        copy.wait()
+
+
+def products(ordered, right):
     return pl.pallas_call(
         product_kernel,
         out_shape=jax.ShapeDtypeStruct((2, NO, NO), jnp.bfloat16),
-        in_specs=[vmem] * 2,
-        out_specs=vmem,
-        compiler_params=pltpu.CompilerParams(vmem_limit_bytes=18 << 20),
-    )(coupling, shifted)
+        in_specs=[VMEM] * 2,
+        out_specs=pl.BlockSpec(memory_space=pl.ANY),
+        scratch_shapes=[
+            pltpu.VMEM((2, NO, NO), jnp.bfloat16),
+            pltpu.SemaphoreType.DMA((2,)),
+        ],
+        compiler_params=PARAMS,
+    )(ordered, right)
 
 
 def shards(green_lesser, coupling, offsets, occupation, transfer_weight, transfer_table):

time: 103 us -> 103 us (level)
  no operation moved by 1% of the time
where the time goes in v6:
time: 103 us
  blocking collectives  80.2 us (78%)
  Pallas kernels  10.7 us (10%)
  waiting for transfers between devices  6.54 us (6%)
  starting transfers between devices  5.28 us (5%)
    all_to_all x1, blocking collectives, shards(): lax.all_to_all(out.reshape(SLICES, NV * DEPTH, NO), PLANE, 0, 0, tiled=True)  55.2 us
    all_to_all x1, blocking collectives, shards(): own = lax.all_to_all(slices, PLANE, 0, 0, tiled=True)  25.1 us
    ppermute x1, waiting for transfers between devices, shards(): lax.ppermute(own[:half], 'z', [(z + 1, z) for z in range(PLANES - 1)])  5.02 us
    ppermute x1, starting transfers between devices, shards(): lax.ppermute(own[half:], 'z', [(z, z + 1) for z in range(PLANES - 1)])  3.36 us
    pallas_call x1, Pallas kernels, mixed_inner(): pl.pallas_call(inner_kernel, out_shape=[MIXED, REST, REST], in_specs=[VME...  3.22 us
    pallas_call x1, Pallas kernels, products(): pl.pallas_call(product_kernel, out_shape=jax.ShapeDtypeStruct((2, NO, NO)...  3.14 us
    pallas_call x2, Pallas kernels, mixed_side(): pl.pallas_call(functools.partial(halo_kernel, side), out_shape=MIXED, in_...  3.01 us
  transfers between devices with their start and end apart: 2, of which 2 were waited for; matrix products, arithmetic and copies ran while one was open for 0% of the time, Pallas kernels for 6%

profile of v6, /device:TPU:129, one launch (start us, length us, event | category | flops | bytes accessed | tf_op | source)
XLA Modules:
  0.0 103.0 jit_solution(16048426346316591831)
XLA Ops:
  0.0 0.0 copy-start.2
  0.0 0.0 copy-start.1
  0.0 0.0 copy-start.4
  0.0 0.0 copy-start.3
  0.0 0.0 copy-start
  0.0 25.1 %all_to_all.10.own = bf16[32,32,512]{2,1,0:T(8,128)(2,1)S(1)} all-to-all(bf16[32,32,512]{2,1,0:T(8,128)(2,1)} %bitcast.6), channel_id=1, replica_groups=mesh['z'=8,'lo'=2,'x'=4,'hi'=2,'core'=2] {'lo','x','hi','core'}, dimensions={0} | all-to-all | bytes 2097152 | tf_op jit(solution)/shard_map/all_to_all | solution.py:198
  25.1 0.1 fusion
  25.2 1.9 %collective-permute-start.1 = (bf16[16,32,512]{2,1,0:T(8,128)(2,1)S(1)}, bf16[16,32,512]{2,1,0:T(8,128)(2,1)S(1)}, u32[]{:S(2)}, u32[]{:S(2)}) collective-permute-start(bf16[16,32,512]{2,1,0:T(8,128)(2,1)S(1)} %get-tuple-element.17), channel_id=1, source_target_pairs={{32,0},{64,32},{96,64},{128,96},{160,128},{192,160},{224,192},{33,... | collective-permute-start | bytes 1572872 | tf_op jit(solution)/shard_map/ppermute | solution.py:201
  27.1 3.4 %collective-permute-start = (bf16[16,32,512]{2,1,0:T(8,128)(2,1)S(1)}, bf16[16,32,512]{2,1,0:T(8,128)(2,1)S(1)}, u32[]{:S(2)}, u32[]{:S(2)}) collective-permute-start(bf16[16,32,512]{2,1,0:T(8,128)(2,1)S(1)} %get-tuple-element.18), channel_id=1, source_target_pairs={{0,32},{32,64},{64,96},{96,128},{128,160},{160,192},{192,224},{1,3... | collective-permute-start | bytes 1572872 | tf_op jit(solution)/shard_map/ppermute | solution.py:200
  30.5 0.0 copy-done.2
  30.5 0.0 copy-done.1
  30.5 0.0 copy-done.4
  30.5 0.0 copy-done.3
  30.5 0.0 copy-done
  30.5 1.3 %shard_map.64 = (bf16[4,256,256]{2,1,0:T(8,128)(2,1)S(1)}, bf16[4,512,512]{2,1,0:T(8,128)(2,1)S(1)}, bf16[4,512,512]{2,1,0:T(8,128)(2,1)S(1)}) custom-call(s32[4]{0:T(128)S(1)} %copy-done.3, f32[4]{0:T(128)S(1)} %copy-done.4, f32[4,4]{1,0:T(4,128)S(1)} %copy-done.1, s32[4,4]{1,0:T(4,128)S(1)} %copy-done.2, bf16[4,512,512]{2,1,0:T(8,128)(2,1)S(1)} %copy-done), custom_call_target="tpu_custom_call" | custom-call | tf_op jit(solution)/shard_map/pallas_call | solution.py:128
  31.8 3.2 %shard_map.65 = (bf16[32,4,32,512]{3,2,1,0:T(8,128)(2,1)S(1)}, f32[10,128,512]{2,1,0:T(8,128)S(1)}, f32[10,128,512]{2,1,0:T(8,128)S(1)}) custom-call(bf16[4,256,256]{2,1,0:T(8,128)(2,1)S(1)} %get-tuple-element.12.scale, bf16[4,512,512]{2,1,0:T(8,128)(2,1)S(1)} %get-tuple-element.13.turned, bf16[32,32,512]{2,1,0:T(8,128)(2,1)S(1)} %all_to_all.10.own), custom_call_target="tpu_custom_call" | custom-call | tf_op jit(solution)/shard_map/pallas_call | solution.py:143
  35.1 5.0 %collective-permute-done.1.halo = bf16[16,32,512]{2,1,0:T(8,128)(2,1)S(1)} collective-permute-done((bf16[16,32,512]{2,1,0:T(8,128)(2,1)S(1)}, bf16[16,32,512]{2,1,0:T(8,128)(2,1)S(1)}, u32[]{:S(2)}, u32[]{:S(2)}) %collective-permute-start.1) | collective-permute-done | bytes 524320 | tf_op jit(solution)/shard_map/ppermute | solution.py:201
  40.1 1.5 %shard_map.66.started = bf16[32,4,32,512]{3,2,1,0:T(8,128)(2,1)S(1)} custom-call(bf16[4,256,256]{2,1,0:T(8,128)(2,1)S(1)} %get-tuple-element.12.scale, bf16[4,512,512]{2,1,0:T(8,128)(2,1)S(1)} %get-tuple-element.13.turned, bf16[16,32,512]{2,1,0:T(8,128)(2,1)S(1)} %collective-permute-done.1.halo, ...), custom_call_target="tpu_custom_call", output_to_operand_aliasing={{}: (4, {})} | custom-call | tf_op jit(solution)/shard_map/pallas_call | solution.py:154
  41.6 1.5 %collective-permute-done.halo = bf16[16,32,512]{2,1,0:T(8,128)(2,1)S(1)} collective-permute-done((bf16[16,32,512]{2,1,0:T(8,128)(2,1)S(1)}, bf16[16,32,512]{2,1,0:T(8,128)(2,1)S(1)}, u32[]{:S(2)}, u32[]{:S(2)}) %collective-permute-start) | collective-permute-done | bytes 524320 | tf_op jit(solution)/shard_map/ppermute | solution.py:200
  43.1 1.5 %shard_map.67 = bf16[32,4,32,512]{3,2,1,0:T(8,128)(2,1)S(1)} custom-call(bf16[4,256,256]{2,1,0:T(8,128)(2,1)S(1)} %get-tuple-element.12.scale, bf16[4,512,512]{2,1,0:T(8,128)(2,1)S(1)} %get-tuple-element.13.turned, bf16[16,32,512]{2,1,0:T(8,128)(2,1)S(1)} %collective-permute-done.halo, ...), custom_call_target="tpu_custom_call", output_to_operand_aliasing={{}: (4, {})} | custom-call | tf_op jit(solution)/shard_map/pallas_call | solution.py:154
  44.6 55.2 %all_to_all.11 = bf16[32,128,512]{2,1,0:T(8,128)(2,1)S(1)} all-to-all(bf16[32,128,512]{2,1,0:T(8,128)(2,1)S(1)} %bitcast.4), channel_id=1, replica_groups=mesh['z'=8,'lo'=2,'x'=4,'hi'=2,'core'=2] {'lo','x','hi','core'}, dimensions={0} | all-to-all | bytes 8388608 | tf_op jit(solution)/shard_map/all_to_all | solution.py:206
  99.8 3.1 %shard_map.68 = bf16[2,512,512]{2,1,0:T(8,128)(2,1)} custom-call(bf16[4,512,512]{2,1,0:T(8,128)(2,1)S(1)} %get-tuple-element.11.ordered, bf16[32,4,32,512]{3,2,1,0:T(8,128)(2,1)S(1)} %bitcast.5), custom_call_target="tpu_custom_call" | custom-call | tf_op jit(solution)/shard_map/pallas_call | solution.py:183
Async XLA Ops:
  0.0 30.5 %copy-start.2 = (s32[4,4]{1,0:T(4,128)S(1)}, s32[4,4]{1,0:T(4,128)}, u32[]{:S(2)}) copy-start(s32[4,4]{1,0:T(4,128)} %table.1) | copy-start | bytes 196
  0.0 30.5 %copy-start.1 = (f32[4,4]{1,0:T(4,128)S(1)}, f32[4,4]{1,0:T(4,128)}, u32[]{:S(2)}) copy-start(f32[4,4]{1,0:T(4,128)} %weight.1) | copy-start | bytes 196
  0.0 30.5 %copy-start.4 = (f32[4]{0:T(128)S(1)}, f32[4]{0:T(128)}, u32[]{:S(2)}) copy-start(f32[4]{0:T(128)} %occupation.1) | copy-start | bytes 52
  0.0 30.5 %copy-start.3 = (s32[4]{0:T(128)S(1)}, s32[4]{0:T(128)}, u32[]{:S(2)}) copy-start(s32[4]{0:T(128)} %offsets.1) | copy-start | bytes 52
  0.0 30.5 %copy-start = (bf16[4,512,512]{2,1,0:T(8,128)(2,1)S(1)}, bf16[4,512,512]{2,1,0:T(8,128)(2,1)}, u32[]{:S(2)}) copy-start(bf16[4,512,512]{2,1,0:T(8,128)(2,1)} %coupling.1) | copy-start | bytes 6291460
  25.2 14.9 %collective-permute-start.1 = (bf16[16,32,512]{2,1,0:T(8,128)(2,1)S(1)}, bf16[16,32,512]{2,1,0:T(8,128)(2,1)S(1)}, u32[]{:S(2)}, u32[]{:S(2)}) collective-permute-start(bf16[16,32,512]{2,1,0:T(8,128)(2,1)S(1)} %get-tuple-element.17), channel_id=1, source_target_pairs={{32,0},{64,32},{96,64},{128,96},{160,128},{192,160},{224,192},{33,... | collective-permute-start | bytes 1572872 | tf_op jit(solution)/shard_map/ppermute | solution.py:201
  27.1 16.0 %collective-permute-start = (bf16[16,32,512]{2,1,0:T(8,128)(2,1)S(1)}, bf16[16,32,512]{2,1,0:T(8,128)(2,1)S(1)}, u32[]{:S(2)}, u32[]{:S(2)}) collective-permute-start(bf16[16,32,512]{2,1,0:T(8,128)(2,1)S(1)} %get-tuple-element.18), channel_id=1, source_target_pairs={{0,32},{32,64},{64,96},{96,128},{128,160},{160,192},{192,224},{1,3... | collective-permute-start | bytes 1572872 | tf_op jit(solution)/shard_map/ppermute | solution.py:200

commit v7 on v6

--- a/solution.py
+++ b/solution.py
@@ -49,9 +49,9 @@
                 scaled = base * (occupation[mode] + float(side))
                 high = scaled.astype(jnp.bfloat16)
                 rest = (scaled - high.astype(jnp.float32)).astype(jnp.bfloat16)
-                columns = slice(side * WIDE, (side + 1) * WIDE)
-                out[dist - 1, k * DEPTH : (k + 1) * DEPTH, columns] = high
-                out[dist - 1, WIDE + k * DEPTH : WIDE + (k + 1) * DEPTH, columns] = rest
+                rows = slice(k * DEPTH, (k + 1) * DEPTH)
+                out[dist - 1, rows, 2 * side * WIDE : (2 * side + 1) * WIDE] = high
+                out[dist - 1, rows, (2 * side + 1) * WIDE : (2 * side + 2) * WIDE] = rest
 
 
 def block(ref, e):
@@ -79,9 +79,9 @@
     return range(NE - dist, NE)
 
 
-def weighted(weights, source):
-    total = jnp.dot(weights, source, preferred_element_type=jnp.float32)
-    return total[:WIDE] + total[WIDE:]
+def weighted(weights, *sources):
+    twice = jnp.concatenate([source for source in sources for _ in range(2)], axis=0)
+    return jnp.dot(weights, twice, preferred_element_type=jnp.float32)
 
 
 def inner_kernel(scale, turned, own, out, low_rest, high_rest, sums):
@@ -89,27 +89,27 @@
         weights = scale[dist - 1]
         energies = range(dist, NE - dist)
         for index, e in enumerate(energies):
-            both = jnp.concatenate([block(own, e - dist), block(own, e + dist)], axis=0)
-            sums[index] = weighted(weights, both).astype(jnp.bfloat16)
+            total = weighted(weights, block(own, e - dist), block(own, e + dist))
+            sums[index] = total.astype(jnp.bfloat16)
         if energies:
             rows = sums[0 : len(energies)].reshape(len(energies) * WIDE, NO)
             times_right(turned, dist, rows, energies, out)
         for index, e in enumerate(below_at(dist)):
-            low_rest[packed(dist) + index] = weighted(weights[:, WIDE:], block(own, e + dist))
+            low_rest[packed(dist) + index] = weighted(weights[:, 2 * WIDE :], block(own, e + dist))
         for index, e in enumerate(above_at(dist)):
-            high_rest[packed(dist) + index] = weighted(weights[:, :WIDE], block(own, e - dist))
+            high_rest[packed(dist) + index] = weighted(weights[:, : 2 * WIDE], block(own, e - dist))
 
 
 def halo_kernel(side, scale, turned, halo, rest, started, out, sums):
     for reach in DISTS:
         source = HALO - reach if side == LOW else reach - 1
-        columns = slice(side * WIDE, (side + 1) * WIDE)
-        weights = scale[reach - 1 :, :, columns].reshape((HALO + 1 - reach) * 2 * WIDE, WIDE)
-        total = jnp.dot(weights, block(halo, source), preferred_element_type=jnp.float32)
+        columns = slice(2 * side * WIDE, (2 * side + 2) * WIDE)
+        weights = scale[reach - 1 :, :, columns].reshape((HALO + 1 - reach) * WIDE, 2 * WIDE)
+        total = weighted(weights, block(halo, source))
         for dist in range(reach, HALO + 1):
             index = packed(dist) + (dist - reach if side == LOW else reach - 1)
-            first = (dist - reach) * 2 * WIDE
-            part = total[first : first + WIDE] + total[first + WIDE : first + 2 * WIDE]
+            first = (dist - reach) * WIDE
+            part = total[first : first + WIDE]
             sums[index] = (rest[index] + part).astype(jnp.bfloat16)
     for dist in DISTS:
         rows = sums[packed(dist) : packed(dist) + dist].reshape(dist * WIDE, NO)
@@ -128,7 +128,7 @@
     return pl.pallas_call(
         weight_kernel,
         out_shape=[
-            jax.ShapeDtypeStruct((HALO, 2 * WIDE, 2 * WIDE), jnp.bfloat16),
+            jax.ShapeDtypeStruct((HALO, WIDE, 4 * WIDE), jnp.bfloat16),
             jax.ShapeDtypeStruct((HALO, NO, NO), jnp.bfloat16),
             jax.ShapeDtypeStruct((HALO, NO, NO), jnp.bfloat16),
         ],

time: 103 us -> 103 us (level)
  Pallas kernels: 10.7 us -> 9.38 us
  transfers between devices with their start and end apart: 2 -> 2, of which waited for: 2 -> 2; matrix products, arithmetic and copies ran while one was open for 0% -> 0% of each run, Pallas kernels for 6% -> 5%
where the time goes in v7:
time: 103 us
  blocking collectives  80.2 us (78%)
  Pallas kernels  9.38 us (9%)
  waiting for transfers between devices  7.52 us (7%)
  starting transfers between devices  5.28 us (5%)
    all_to_all x1, blocking collectives, shards(): lax.all_to_all(out.reshape(SLICES, NV * DEPTH, NO), PLANE, 0, 0, tiled=True)  55.2 us
    all_to_all x1, blocking collectives, shards(): own = lax.all_to_all(slices, PLANE, 0, 0, tiled=True)  25.1 us
    ppermute x1, waiting for transfers between devices, shards(): lax.ppermute(own[:half], 'z', [(z + 1, z) for z in range(PLANES - 1)])  5.69 us
    ppermute x1, starting transfers between devices, shards(): lax.ppermute(own[half:], 'z', [(z, z + 1) for z in range(PLANES - 1)])  3.36 us
    pallas_call x1, Pallas kernels, products(): pl.pallas_call(product_kernel, out_shape=jax.ShapeDtypeStruct((2, NO, NO)...  3.14 us
    pallas_call x1, Pallas kernels, mixed_inner(): pl.pallas_call(inner_kernel, out_shape=[MIXED, REST, REST], in_specs=[VME...  2.57 us
    pallas_call x2, Pallas kernels, mixed_side(): pl.pallas_call(functools.partial(halo_kernel, side), out_shape=MIXED, in_...  2.38 us
  transfers between devices with their start and end apart: 2, of which 2 were waited for; matrix products, arithmetic and copies ran while one was open for 0% of the time, Pallas kernels for 5%

profile of v7, /device:TPU:129, one launch (start us, length us, event | category | flops | bytes accessed | tf_op | source)
XLA Modules:
  0.0 102.6 jit_solution(13686255588778463914)
XLA Ops:
  0.0 0.0 copy-start.2
  0.0 0.0 copy-start.1
  0.0 0.0 copy-start.4
  0.0 0.0 copy-start.3
  0.0 0.0 copy-start
  0.0 25.1 %all_to_all.10.own = bf16[32,32,512]{2,1,0:T(8,128)(2,1)S(1)} all-to-all(bf16[32,32,512]{2,1,0:T(8,128)(2,1)} %bitcast.6), channel_id=1, replica_groups=mesh['z'=8,'lo'=2,'x'=4,'hi'=2,'core'=2] {'lo','x','hi','core'}, dimensions={0} | all-to-all | bytes 2097152 | tf_op jit(solution)/shard_map/all_to_all | solution.py:198
  25.1 0.1 fusion
  25.2 1.9 %collective-permute-start.1 = (bf16[16,32,512]{2,1,0:T(8,128)(2,1)S(1)}, bf16[16,32,512]{2,1,0:T(8,128)(2,1)S(1)}, u32[]{:S(2)}, u32[]{:S(2)}) collective-permute-start(bf16[16,32,512]{2,1,0:T(8,128)(2,1)S(1)} %get-tuple-element.17), channel_id=1, source_target_pairs={{32,0},{64,32},{96,64},{128,96},{160,128},{192,160},{224,192},{33,... | collective-permute-start | bytes 1572872 | tf_op jit(solution)/shard_map/ppermute | solution.py:201
  27.1 3.4 %collective-permute-start = (bf16[16,32,512]{2,1,0:T(8,128)(2,1)S(1)}, bf16[16,32,512]{2,1,0:T(8,128)(2,1)S(1)}, u32[]{:S(2)}, u32[]{:S(2)}) collective-permute-start(bf16[16,32,512]{2,1,0:T(8,128)(2,1)S(1)} %get-tuple-element.18), channel_id=1, source_target_pairs={{0,32},{32,64},{64,96},{96,128},{128,160},{160,192},{192,224},{1,3... | collective-permute-start | bytes 1572872 | tf_op jit(solution)/shard_map/ppermute | solution.py:200
  30.5 0.0 copy-done.2
  30.5 0.0 copy-done.1
  30.5 0.0 copy-done.4
  30.5 0.0 copy-done.3
  30.5 0.0 copy-done
  30.5 1.3 %shard_map.64 = (bf16[4,128,512]{2,1,0:T(8,128)(2,1)S(1)}, bf16[4,512,512]{2,1,0:T(8,128)(2,1)S(1)}, bf16[4,512,512]{2,1,0:T(8,128)(2,1)S(1)}) custom-call(s32[4]{0:T(128)S(1)} %copy-done.3, f32[4]{0:T(128)S(1)} %copy-done.4, f32[4,4]{1,0:T(4,128)S(1)} %copy-done.1, s32[4,4]{1,0:T(4,128)S(1)} %copy-done.2, bf16[4,512,512]{2,1,0:T(8,128)(2,1)S(1)} %copy-done), custom_call_target="tpu_custom_call" | custom-call | tf_op jit(solution)/shard_map/pallas_call | solution.py:128
  31.8 2.6 %shard_map.65 = (bf16[32,4,32,512]{3,2,1,0:T(8,128)(2,1)S(1)}, f32[10,128,512]{2,1,0:T(8,128)S(1)}, f32[10,128,512]{2,1,0:T(8,128)S(1)}) custom-call(bf16[4,128,512]{2,1,0:T(8,128)(2,1)S(1)} %get-tuple-element.12.scale, bf16[4,512,512]{2,1,0:T(8,128)(2,1)S(1)} %get-tuple-element.13.turned, bf16[32,32,512]{2,1,0:T(8,128)(2,1)S(1)} %all_to_all.10.own), custom_call_target="tpu_custom_call" | custom-call | tf_op jit(solution)/shard_map/pallas_call | solution.py:143
  34.4 5.7 %collective-permute-done.1.halo = bf16[16,32,512]{2,1,0:T(8,128)(2,1)S(1)} collective-permute-done((bf16[16,32,512]{2,1,0:T(8,128)(2,1)S(1)}, bf16[16,32,512]{2,1,0:T(8,128)(2,1)S(1)}, u32[]{:S(2)}, u32[]{:S(2)}) %collective-permute-start.1) | collective-permute-done | bytes 524320 | tf_op jit(solution)/shard_map/ppermute | solution.py:201
  40.1 1.2 %shard_map.66.started = bf16[32,4,32,512]{3,2,1,0:T(8,128)(2,1)S(1)} custom-call(bf16[4,128,512]{2,1,0:T(8,128)(2,1)S(1)} %get-tuple-element.12.scale, bf16[4,512,512]{2,1,0:T(8,128)(2,1)S(1)} %get-tuple-element.13.turned, bf16[16,32,512]{2,1,0:T(8,128)(2,1)S(1)} %collective-permute-done.1.halo, ...), custom_call_target="tpu_custom_call", output_to_operand_aliasing={{}: (4, {})} | custom-call | tf_op jit(solution)/shard_map/pallas_call | solution.py:154
  41.3 1.8 %collective-permute-done.halo = bf16[16,32,512]{2,1,0:T(8,128)(2,1)S(1)} collective-permute-done((bf16[16,32,512]{2,1,0:T(8,128)(2,1)S(1)}, bf16[16,32,512]{2,1,0:T(8,128)(2,1)S(1)}, u32[]{:S(2)}, u32[]{:S(2)}) %collective-permute-start) | collective-permute-done | bytes 524320 | tf_op jit(solution)/shard_map/ppermute | solution.py:200
  43.1 1.2 %shard_map.67 = bf16[32,4,32,512]{3,2,1,0:T(8,128)(2,1)S(1)} custom-call(bf16[4,128,512]{2,1,0:T(8,128)(2,1)S(1)} %get-tuple-element.12.scale, bf16[4,512,512]{2,1,0:T(8,128)(2,1)S(1)} %get-tuple-element.13.turned, bf16[16,32,512]{2,1,0:T(8,128)(2,1)S(1)} %collective-permute-done.halo, ...), custom_call_target="tpu_custom_call", output_to_operand_aliasing={{}: (4, {})} | custom-call | tf_op jit(solution)/shard_map/pallas_call | solution.py:154
  44.3 55.2 %all_to_all.11 = bf16[32,128,512]{2,1,0:T(8,128)(2,1)S(1)} all-to-all(bf16[32,128,512]{2,1,0:T(8,128)(2,1)S(1)} %bitcast.4), channel_id=1, replica_groups=mesh['z'=8,'lo'=2,'x'=4,'hi'=2,'core'=2] {'lo','x','hi','core'}, dimensions={0} | all-to-all | bytes 8388608 | tf_op jit(solution)/shard_map/all_to_all | solution.py:206
  99.5 3.1 %shard_map.68 = bf16[2,512,512]{2,1,0:T(8,128)(2,1)} custom-call(bf16[4,512,512]{2,1,0:T(8,128)(2,1)S(1)} %get-tuple-element.11.ordered, bf16[32,4,32,512]{3,2,1,0:T(8,128)(2,1)S(1)} %bitcast.5), custom_call_target="tpu_custom_call" | custom-call | tf_op jit(solution)/shard_map/pallas_call | solution.py:183
Async XLA Ops:
  0.0 30.5 %copy-start.2 = (s32[4,4]{1,0:T(4,128)S(1)}, s32[4,4]{1,0:T(4,128)}, u32[]{:S(2)}) copy-start(s32[4,4]{1,0:T(4,128)} %table.1) | copy-start | bytes 196
  0.0 30.5 %copy-start.1 = (f32[4,4]{1,0:T(4,128)S(1)}, f32[4,4]{1,0:T(4,128)}, u32[]{:S(2)}) copy-start(f32[4,4]{1,0:T(4,128)} %weight.1) | copy-start | bytes 196
  0.0 30.5 %copy-start.4 = (f32[4]{0:T(128)S(1)}, f32[4]{0:T(128)}, u32[]{:S(2)}) copy-start(f32[4]{0:T(128)} %occupation.1) | copy-start | bytes 52
  0.0 30.5 %copy-start.3 = (s32[4]{0:T(128)S(1)}, s32[4]{0:T(128)}, u32[]{:S(2)}) copy-start(s32[4]{0:T(128)} %offsets.1) | copy-start | bytes 52
  0.0 30.5 %copy-start = (bf16[4,512,512]{2,1,0:T(8,128)(2,1)S(1)}, bf16[4,512,512]{2,1,0:T(8,128)(2,1)}, u32[]{:S(2)}) copy-start(bf16[4,512,512]{2,1,0:T(8,128)(2,1)} %coupling.1) | copy-start | bytes 6291460
  25.2 14.9 %collective-permute-start.1 = (bf16[16,32,512]{2,1,0:T(8,128)(2,1)S(1)}, bf16[16,32,512]{2,1,0:T(8,128)(2,1)S(1)}, u32[]{:S(2)}, u32[]{:S(2)}) collective-permute-start(bf16[16,32,512]{2,1,0:T(8,128)(2,1)S(1)} %get-tuple-element.17), channel_id=1, source_target_pairs={{32,0},{64,32},{96,64},{128,96},{160,128},{192,160},{224,192},{33,... | collective-permute-start | bytes 1572872 | tf_op jit(solution)/shard_map/ppermute | solution.py:201
  27.1 16.0 %collective-permute-start = (bf16[16,32,512]{2,1,0:T(8,128)(2,1)S(1)}, bf16[16,32,512]{2,1,0:T(8,128)(2,1)S(1)}, u32[]{:S(2)}, u32[]{:S(2)}) collective-permute-start(bf16[16,32,512]{2,1,0:T(8,128)(2,1)S(1)} %get-tuple-element.18), channel_id=1, source_target_pairs={{0,32},{32,64},{64,96},{96,128},{128,160},{160,192},{192,224},{1,3... | collective-permute-start | bytes 1572872 | tf_op jit(solution)/shard_map/ppermute | solution.py:200

commit v8 on v7

--- a/solution.py
+++ b/solution.py
@@ -171,10 +171,13 @@
             rows = right[part * half : part * half + half, index].reshape(NO, NO)
             term = jnp.dot(ordered[index], rows, preferred_element_type=jnp.float32)
             total = term if total is None else total + term
-        ready[part] = total.astype(jnp.bfloat16)
-        copy = pltpu.make_async_copy(ready.at[part], out.at[part], sems.at[part])
-        copy.start()
-        copies.append(copy)
+        for index in range(2):
+            rows = slice(index * NO // 2, (index + 1) * NO // 2)
+            ready[part, rows] = total[rows].astype(jnp.bfloat16)
+            place = (part, pl.ds(index * NO // 2, NO // 2))
+            copy = pltpu.make_async_copy(ready.at[place], out.at[place], sems.at[part, index])
+            copy.start()
+            copies.append(copy)
     for copy in copies:
         copy.wait()
 
@@ -187,7 +190,7 @@
         out_specs=pl.BlockSpec(memory_space=pl.ANY),
         scratch_shapes=[
             pltpu.VMEM((2, NO, NO), jnp.bfloat16),
-            pltpu.SemaphoreType.DMA((2,)),
+            pltpu.SemaphoreType.DMA((2, 2)),
         ],
         compiler_params=PARAMS,
     )(ordered, right)

time: 103 us -> 103 us (level)
  no operation moved by 1% of the time
where the time goes in v8:
time: 103 us
  blocking collectives  80.2 us (78%)
  Pallas kernels  9.33 us (9%)
  waiting for transfers between devices  7.52 us (7%)
  starting transfers between devices  5.28 us (5%)
    all_to_all x1, blocking collectives, shards(): lax.all_to_all(out.reshape(SLICES, NV * DEPTH, NO), PLANE, 0, 0, tiled=True)  55.2 us
    all_to_all x1, blocking collectives, shards(): own = lax.all_to_all(slices, PLANE, 0, 0, tiled=True)  25.1 us
    ppermute x1, waiting for transfers between devices, shards(): lax.ppermute(own[:half], 'z', [(z + 1, z) for z in range(PLANES - 1)])  5.69 us
    ppermute x1, starting transfers between devices, shards(): lax.ppermute(own[half:], 'z', [(z, z + 1) for z in range(PLANES - 1)])  3.36 us
    pallas_call x1, Pallas kernels, products(): pl.pallas_call(product_kernel, out_shape=jax.ShapeDtypeStruct((2, NO, NO)...  3.08 us
    pallas_call x1, Pallas kernels, mixed_inner(): pl.pallas_call(inner_kernel, out_shape=[MIXED, REST, REST], in_specs=[VME...  2.57 us
    pallas_call x2, Pallas kernels, mixed_side(): pl.pallas_call(functools.partial(halo_kernel, side), out_shape=MIXED, in_...  2.38 us
  transfers between devices with their start and end apart: 2, of which 2 were waited for; matrix products, arithmetic and copies ran while one was open for 0% of the time, Pallas kernels for 5%

profile of v8, /device:TPU:129, one launch (start us, length us, event | category | flops | bytes accessed | tf_op | source)
XLA Modules:
  0.0 102.6 jit_solution(1628746512239665877)
XLA Ops:
  0.0 0.0 copy-start.2
  0.0 0.0 copy-start.1
  0.0 0.0 copy-start.4
  0.0 0.0 copy-start.3
  0.0 0.0 copy-start
  0.0 25.1 %all_to_all.10.own = bf16[32,32,512]{2,1,0:T(8,128)(2,1)S(1)} all-to-all(bf16[32,32,512]{2,1,0:T(8,128)(2,1)} %bitcast.6), channel_id=1, replica_groups=mesh['z'=8,'lo'=2,'x'=4,'hi'=2,'core'=2] {'lo','x','hi','core'}, dimensions={0} | all-to-all | bytes 2097152 | tf_op jit(solution)/shard_map/all_to_all | solution.py:201
  25.1 0.1 fusion
  25.2 1.9 %collective-permute-start.1 = (bf16[16,32,512]{2,1,0:T(8,128)(2,1)S(1)}, bf16[16,32,512]{2,1,0:T(8,128)(2,1)S(1)}, u32[]{:S(2)}, u32[]{:S(2)}) collective-permute-start(bf16[16,32,512]{2,1,0:T(8,128)(2,1)S(1)} %get-tuple-element.17), channel_id=1, source_target_pairs={{32,0},{64,32},{96,64},{128,96},{160,128},{192,160},{224,192},{33,... | collective-permute-start | bytes 1572872 | tf_op jit(solution)/shard_map/ppermute | solution.py:204
  27.1 3.4 %collective-permute-start = (bf16[16,32,512]{2,1,0:T(8,128)(2,1)S(1)}, bf16[16,32,512]{2,1,0:T(8,128)(2,1)S(1)}, u32[]{:S(2)}, u32[]{:S(2)}) collective-permute-start(bf16[16,32,512]{2,1,0:T(8,128)(2,1)S(1)} %get-tuple-element.18), channel_id=1, source_target_pairs={{0,32},{32,64},{64,96},{96,128},{128,160},{160,192},{192,224},{1,3... | collective-permute-start | bytes 1572872 | tf_op jit(solution)/shard_map/ppermute | solution.py:203
  30.5 0.0 copy-done.2
  30.5 0.0 copy-done.1
  30.5 0.0 copy-done.4
  30.5 0.0 copy-done.3
  30.5 0.0 copy-done
  30.5 1.3 %shard_map.64 = (bf16[4,128,512]{2,1,0:T(8,128)(2,1)S(1)}, bf16[4,512,512]{2,1,0:T(8,128)(2,1)S(1)}, bf16[4,512,512]{2,1,0:T(8,128)(2,1)S(1)}) custom-call(s32[4]{0:T(128)S(1)} %copy-done.3, f32[4]{0:T(128)S(1)} %copy-done.4, f32[4,4]{1,0:T(4,128)S(1)} %copy-done.1, s32[4,4]{1,0:T(4,128)S(1)} %copy-done.2, bf16[4,512,512]{2,1,0:T(8,128)(2,1)S(1)} %copy-done), custom_call_target="tpu_custom_call" | custom-call | tf_op jit(solution)/shard_map/pallas_call | solution.py:128
  31.8 2.6 %shard_map.65 = (bf16[32,4,32,512]{3,2,1,0:T(8,128)(2,1)S(1)}, f32[10,128,512]{2,1,0:T(8,128)S(1)}, f32[10,128,512]{2,1,0:T(8,128)S(1)}) custom-call(bf16[4,128,512]{2,1,0:T(8,128)(2,1)S(1)} %get-tuple-element.12.scale, bf16[4,512,512]{2,1,0:T(8,128)(2,1)S(1)} %get-tuple-element.13.turned, bf16[32,32,512]{2,1,0:T(8,128)(2,1)S(1)} %all_to_all.10.own), custom_call_target="tpu_custom_call" | custom-call | tf_op jit(solution)/shard_map/pallas_call | solution.py:143
  34.4 5.7 %collective-permute-done.1.halo = bf16[16,32,512]{2,1,0:T(8,128)(2,1)S(1)} collective-permute-done((bf16[16,32,512]{2,1,0:T(8,128)(2,1)S(1)}, bf16[16,32,512]{2,1,0:T(8,128)(2,1)S(1)}, u32[]{:S(2)}, u32[]{:S(2)}) %collective-permute-start.1) | collective-permute-done | bytes 524320 | tf_op jit(solution)/shard_map/ppermute | solution.py:204
  40.1 1.2 %shard_map.66.started = bf16[32,4,32,512]{3,2,1,0:T(8,128)(2,1)S(1)} custom-call(bf16[4,128,512]{2,1,0:T(8,128)(2,1)S(1)} %get-tuple-element.12.scale, bf16[4,512,512]{2,1,0:T(8,128)(2,1)S(1)} %get-tuple-element.13.turned, bf16[16,32,512]{2,1,0:T(8,128)(2,1)S(1)} %collective-permute-done.1.halo, ...), custom_call_target="tpu_custom_call", output_to_operand_aliasing={{}: (4, {})} | custom-call | tf_op jit(solution)/shard_map/pallas_call | solution.py:154
  41.3 1.8 %collective-permute-done.halo = bf16[16,32,512]{2,1,0:T(8,128)(2,1)S(1)} collective-permute-done((bf16[16,32,512]{2,1,0:T(8,128)(2,1)S(1)}, bf16[16,32,512]{2,1,0:T(8,128)(2,1)S(1)}, u32[]{:S(2)}, u32[]{:S(2)}) %collective-permute-start) | collective-permute-done | bytes 524320 | tf_op jit(solution)/shard_map/ppermute | solution.py:203
  43.1 1.2 %shard_map.67 = bf16[32,4,32,512]{3,2,1,0:T(8,128)(2,1)S(1)} custom-call(bf16[4,128,512]{2,1,0:T(8,128)(2,1)S(1)} %get-tuple-element.12.scale, bf16[4,512,512]{2,1,0:T(8,128)(2,1)S(1)} %get-tuple-element.13.turned, bf16[16,32,512]{2,1,0:T(8,128)(2,1)S(1)} %collective-permute-done.halo, ...), custom_call_target="tpu_custom_call", output_to_operand_aliasing={{}: (4, {})} | custom-call | tf_op jit(solution)/shard_map/pallas_call | solution.py:154
  44.3 55.2 %all_to_all.11 = bf16[32,128,512]{2,1,0:T(8,128)(2,1)S(1)} all-to-all(bf16[32,128,512]{2,1,0:T(8,128)(2,1)S(1)} %bitcast.4), channel_id=1, replica_groups=mesh['z'=8,'lo'=2,'x'=4,'hi'=2,'core'=2] {'lo','x','hi','core'}, dimensions={0} | all-to-all | bytes 8388608 | tf_op jit(solution)/shard_map/all_to_all | solution.py:209
  99.5 3.1 %shard_map.68 = bf16[2,512,512]{2,1,0:T(8,128)(2,1)} custom-call(bf16[4,512,512]{2,1,0:T(8,128)(2,1)S(1)} %get-tuple-element.11.ordered, bf16[32,4,32,512]{3,2,1,0:T(8,128)(2,1)S(1)} %bitcast.5), custom_call_target="tpu_custom_call" | custom-call | tf_op jit(solution)/shard_map/pallas_call | solution.py:186
Async XLA Ops:
  0.0 30.5 %copy-start.2 = (s32[4,4]{1,0:T(4,128)S(1)}, s32[4,4]{1,0:T(4,128)}, u32[]{:S(2)}) copy-start(s32[4,4]{1,0:T(4,128)} %table.1) | copy-start | bytes 196
  0.0 30.5 %copy-start.1 = (f32[4,4]{1,0:T(4,128)S(1)}, f32[4,4]{1,0:T(4,128)}, u32[]{:S(2)}) copy-start(f32[4,4]{1,0:T(4,128)} %weight.1) | copy-start | bytes 196
  0.0 30.5 %copy-start.4 = (f32[4]{0:T(128)S(1)}, f32[4]{0:T(128)}, u32[]{:S(2)}) copy-start(f32[4]{0:T(128)} %occupation.1) | copy-start | bytes 52
  0.0 30.5 %copy-start.3 = (s32[4]{0:T(128)S(1)}, s32[4]{0:T(128)}, u32[]{:S(2)}) copy-start(s32[4]{0:T(128)} %offsets.1) | copy-start | bytes 52
  0.0 30.5 %copy-start = (bf16[4,512,512]{2,1,0:T(8,128)(2,1)S(1)}, bf16[4,512,512]{2,1,0:T(8,128)(2,1)}, u32[]{:S(2)}) copy-start(bf16[4,512,512]{2,1,0:T(8,128)(2,1)} %coupling.1) | copy-start | bytes 6291460
  25.2 14.9 %collective-permute-start.1 = (bf16[16,32,512]{2,1,0:T(8,128)(2,1)S(1)}, bf16[16,32,512]{2,1,0:T(8,128)(2,1)S(1)}, u32[]{:S(2)}, u32[]{:S(2)}) collective-permute-start(bf16[16,32,512]{2,1,0:T(8,128)(2,1)S(1)} %get-tuple-element.17), channel_id=1, source_target_pairs={{32,0},{64,32},{96,64},{128,96},{160,128},{192,160},{224,192},{33,... | collective-permute-start | bytes 1572872 | tf_op jit(solution)/shard_map/ppermute | solution.py:204
  27.1 16.0 %collective-permute-start = (bf16[16,32,512]{2,1,0:T(8,128)(2,1)S(1)}, bf16[16,32,512]{2,1,0:T(8,128)(2,1)S(1)}, u32[]{:S(2)}, u32[]{:S(2)}) collective-permute-start(bf16[16,32,512]{2,1,0:T(8,128)(2,1)S(1)} %get-tuple-element.18), channel_id=1, source_target_pairs={{0,32},{32,64},{64,96},{96,128},{128,160},{160,192},{192,224},{1,3... | collective-permute-start | bytes 1572872 | tf_op jit(solution)/shard_map/ppermute | solution.py:203
